TPU v7x, 256 devices: a whole 4x4x8 slice. The times are simulated.
256 devices in a mesh: roll: 4 (over y), exp: 64 (over x, z, core).
Axes of the slice: x: 4, y: 4, z: 8, core: 2. Of those that a mesh axis runs over, the one named last changes fastest.
Arguments:
- tokens: bfloat16 [2048, 4096], P(('roll', 'exp')), may hold values from -6 to 6
- cotangent: bfloat16 [2048, 4096], P(('roll', 'exp')), may hold values from -6 to 6
- router_probs: bfloat16 [2048, 8], P(('roll', 'exp')), may hold values from 0.019897461 to 0.5
- expert_ids: int32 [2048, 8], P(('roll', 'exp')), may hold values from 0 to 63, all different within a row; in each aligned block of 8 rows (0 to 7, 8 to 15, ...) at most 2 rows name the same one
- rewards: int32 [64, 16], P('exp', 'roll'), may hold values from 0 to 12
- lengths: int32 [64, 16], P('exp', 'roll'), may hold values from 256 to 1024
- gate_weight: bfloat16 [64, 4096, 1536], P('exp', None, 'roll'), may hold values from -0.09375 to 0.09375
- up_weight: bfloat16 [64, 4096, 1536], P('exp', None, 'roll'), may hold values from -0.09375 to 0.09375
- down_weight: bfloat16 [64, 1536, 4096], P('exp', 'roll'), may hold values from -0.15625 to 0.15625
Outputs:
- grad_tokens: bfloat16 [2048, 4096], P(('roll', 'exp'))
- grad_probs: bfloat16 [2048, 8], P(('roll', 'exp'))
- grad_down: bfloat16 [64, 1536, 4096], P('exp', 'roll')
Inputs may be any that keep to these rules, and one draw needn't show every extreme that they name: `expert_ids`: within the rows of one device no expert is named more than 2 times, a bound that some block reaches.
All inputs are finite; a program needn't handle non-finite values.
Results may differ from a plain program's by a relative error of at most 0.0065.
Values may be sent and summed in bfloat16 or wider, within the bound.
No kernel may reach another device: no remote copies, remote signals or barrier semaphores. Data moves between devices by JAX's collectives and lax.ppermute only.
A program may use at most 128 MiB of HBM per device.

v0:
```python
import jax
import jax.numpy as jnp
from jax import lax
from jax.sharding import PartitionSpec as P


def silu_parts(pre_value):
    sigmoid_value = jax.nn.sigmoid(pre_value)
    return (pre_value * sigmoid_value, sigmoid_value * (1.0 + pre_value * (1.0 - sigmoid_value)))


def make_slots(id_blocks, experts, capacity):
    blocks, tok_count, top_count = id_blocks.shape
    chosen = (id_blocks[..., None] == jnp.arange(experts, dtype=jnp.int32)).astype(jnp.float32)
    flat_chosen = chosen.reshape(blocks, tok_count * top_count, experts)
    ranking = jnp.cumsum(flat_chosen, axis=1) - flat_chosen
    layout = flat_chosen[..., None] * (
        ranking[..., None] == jnp.arange(capacity, dtype=jnp.float32)
    ).astype(jnp.float32)
    return layout.reshape(blocks, tok_count, top_count, experts, capacity)


def pack_rows(layout, tok_rows, grad_rows, prob_rows):
    per_token = jnp.sum(layout, axis=2).astype(jnp.bfloat16)
    row_block = jnp.einsum(
        "btec,btd->ebcd", per_token, tok_rows, preferred_element_type=jnp.float32
    ).astype(jnp.bfloat16)
    grad_block = jnp.einsum(
        "btec,btd->ebcd", per_token, grad_rows, preferred_element_type=jnp.float32
    ).astype(jnp.bfloat16)
    prob_block = jnp.einsum("btkec,btk->ebc", layout, prob_rows.astype(jnp.float32)).astype(
        jnp.bfloat16
    )
    return (row_block, grad_block, prob_block)


def on_device(
    tokens,
    cotangent,
    router_probs,
    expert_ids,
    rewards,
    lengths,
    gate_weight,
    up_weight,
    down_weight,
):
    experts = lax.axis_size("exp")
    n_roll = lax.axis_size("roll")
    tok_count = tokens.shape[0]
    top_count = expert_ids.shape[1]
    capacity = min(tok_count, max(2, 2 * tok_count * top_count // experts))
    reward_f = rewards.astype(jnp.float32)
    length_f = lengths.astype(jnp.float32)
    totals, squares, spans = lax.psum(
        (
            jnp.sum(reward_f, axis=1),
            jnp.sum(reward_f * reward_f, axis=1),
            jnp.sum(length_f, axis=1),
        ),
        "roll",
    )
    group_size = rewards.shape[1] * n_roll
    mean_reward = totals / group_size
    spread = jnp.sqrt(squares / group_size - mean_reward * mean_reward)
    advantage = (reward_f - mean_reward[:, None]) / jnp.maximum(spread, 1.0)[:, None]
    weights = advantage * (spans / group_size)[:, None] / length_f
    per_response = tok_count // rewards.shape[1]
    token_weight = jnp.repeat(weights[0], per_response)
    scaled = (token_weight[:, None] * cotangent.astype(jnp.float32)).astype(jnp.bfloat16)
    own_layout = make_slots(expert_ids[None], experts, capacity)
    row_block, grad_block, prob_block = pack_rows(
        own_layout, tokens[None], scaled[None], router_probs[None]
    )
    sent_rows, sent_grads, sent_probs = (
        lax.all_to_all(row_block, "exp", split_axis=0, concat_axis=0, tiled=True),
        lax.all_to_all(grad_block, "exp", split_axis=0, concat_axis=0, tiled=True),
        lax.all_to_all(prob_block, "exp", split_axis=0, concat_axis=0, tiled=True),
    )
    rows_in, grads_in, probs_in = (
        lax.all_gather(sent_rows, "roll", axis=1, tiled=True),
        lax.all_gather(sent_grads, "roll", axis=1, tiled=True),
        lax.all_gather(sent_probs, "roll", axis=1, tiled=True),
    )
    n_source, n_block, cap_in, width = rows_in.shape
    row_total = n_source * n_block * cap_in
    flat_rows = rows_in.reshape(row_total, width)
    flat_grads = grads_in.reshape(row_total, width)
    flat_probs = probs_in.reshape(row_total, 1).astype(jnp.float32)
    w_gate = gate_weight[0]
    w_up = up_weight[0]
    w_down = down_weight[0]
    contract_last = (((1,), (1,)), ((), ()))
    pre_gate = jnp.dot(flat_rows, w_gate, preferred_element_type=jnp.float32)
    pre_up = jnp.dot(flat_rows, w_up, preferred_element_type=jnp.float32)
    activated, slope = silu_parts(pre_gate)
    hidden = (activated * pre_up).astype(jnp.bfloat16)
    back_hidden = lax.dot_general(
        flat_grads, w_down, contract_last, preferred_element_type=jnp.float32
    )
    hidden_grad = flat_probs * back_hidden
    gate_grad = (hidden_grad * pre_up * slope).astype(jnp.bfloat16)
    up_grad = (hidden_grad * activated).astype(jnp.bfloat16)
    input_part = lax.dot_general(
        gate_grad, w_gate, contract_last, preferred_element_type=jnp.float32
    ) + lax.dot_general(up_grad, w_up, contract_last, preferred_element_type=jnp.float32)
    input_part = input_part.reshape(n_source, n_block, cap_in, width)
    weighted = (flat_probs * hidden.astype(jnp.float32)).astype(jnp.bfloat16)
    down_grad = lax.dot_general(
        weighted, flat_grads, (((0,), (0,)), ((), ())), preferred_element_type=jnp.float32
    )
    out_part = jnp.dot(hidden, w_down, preferred_element_type=jnp.float32).reshape(
        n_source, n_block, cap_in, width
    )
    out_own = lax.psum_scatter(out_part, "roll", scatter_dimension=1, tiled=True)
    grad_own = lax.dynamic_index_in_dim(grads_in, lax.axis_index("roll"), 1, keepdims=True)
    prob_own = jnp.sum(out_own * grad_own.astype(jnp.float32), axis=3)
    input_own = lax.psum_scatter(input_part, "roll", scatter_dimension=1, tiled=True)
    grad_back, prob_back = (
        lax.all_to_all(
            input_own.astype(jnp.bfloat16), "exp", split_axis=0, concat_axis=0, tiled=True
        ),
        lax.all_to_all(
            prob_own.astype(jnp.bfloat16), "exp", split_axis=0, concat_axis=0, tiled=True
        ),
    )
    per_token = jnp.sum(own_layout, axis=2).astype(jnp.bfloat16)
    grad_tokens = jnp.einsum(
        "btec,ebcd->btd", per_token, grad_back, preferred_element_type=jnp.float32
    )[0].astype(jnp.bfloat16)
    grad_probs = jnp.einsum("btkec,ebc->btk", own_layout, prob_back.astype(jnp.float32))[0].astype(
        jnp.bfloat16
    )
    return (grad_tokens, grad_probs, down_grad.astype(jnp.bfloat16)[None])


def solution(mesh):
    in_specs = (
        P(("roll", "exp"), None),
        P(("roll", "exp"), None),
        P(("roll", "exp"), None),
        P(("roll", "exp"), None),
        P("exp", "roll"),
        P("exp", "roll"),
        P("exp", None, "roll"),
        P("exp", None, "roll"),
        P("exp", "roll", None),
    )
    out_specs = (P(("roll", "exp"), None), P(("roll", "exp"), None), P("exp", "roll", None))
    return jax.shard_map(
        on_device, mesh=mesh, in_specs=in_specs, out_specs=out_specs, check_vma=False
    )
```

profile of v0, /device:TPU:1, one launch (start us, length us, event | category | flops | bytes accessed | tf_op | source)
XLA Modules:
  0.0 382.4 jit_solution(9730842915692252837)
XLA Ops:
  7.2 0.0 copy-start
  7.2 0.0 all-gather.5.cloned.1.call-start
  7.2 0.9 eq.70
  8.1 0.8 fusion.42
  8.9 0.9 fusion.53
  9.8 0.8 bitcast_subtract_fusion
  10.6 0.6 copy-done.7
  11.2 1.3 fusion.2
  12.6 1.1 copy.92
  13.7 41.5 %all_to_all.25 = bf16[64,1,2,4096]{3,2,1,0:T(2,128)(2,1)S(1)} all-to-all(bf16[64,1,2,4096]{3,2,1,0:T(2,128)(2,1)S(1)} %copy.92), channel_id=1, replica_groups=mesh['roll'=4,'exp'=64] {'exp'}, dimensions={0} | all-to-all | bytes 2097152 | tf_op jit(solution)/shard_map/all_to_all | solution.py:76
  55.2 1.6 copy.93
  56.7 0.0 all-gather.5.cloned.1.call-update
  56.7 0.0 all-gather.3.cloned.1.call-start
  56.8 0.6 convert_reduce_fusion
  57.4 0.7 convert_reduce_fusion.1
  58.1 9.4 %all-reduce = (f32[1]{0:T(128)}, f32[1]{0:T(128)}, f32[1]{0:T(128)}) all-reduce(f32[1]{0:T(128)} %bitcast.7, f32[1]{0:T(128)} %bitcast.5, f32[1]{0:T(128)} %bitcast.3), channel_id=1, replica_groups=mesh['roll'=4,'exp'=64] {'roll'}, use_global_device_ids=true, to_apply=%region_7.8 | all-reduce | flops 3 | bytes 24 | tf_op jit(solution)/shard_map/psum | solution.py:55
  70.6 0.1 broadcast_in_dim.4
  70.7 0.1 mul.89
  70.8 0.5 fusion.1
  71.3 1.1 copy.88
  72.4 36.6 %all_to_all.26 = bf16[64,1,2,4096]{3,2,1,0:T(2,128)(2,1)S(1)} all-to-all(bf16[64,1,2,4096]{3,2,1,0:T(2,128)(2,1)S(1)} %copy.88), channel_id=1, replica_groups=mesh['roll'=4,'exp'=64] {'exp'}, dimensions={0} | all-to-all | bytes 2097152 | tf_op jit(solution)/shard_map/all_to_all | solution.py:77
  108.9 1.6 copy.89
  110.5 0.0 all-gather.3.cloned.1.call-update
  110.6 0.2 reduce-scatter.5.cloned.1.call-start
  110.8 0.0 all-gather.5.cloned.1.call-done
  110.8 8.5 %copy.94 = bf16[64,4,2,4096]{3,2,1,0:T(2,128)(2,1)} copy(bf16[64,4,2,4096]{3,0,2,1:T(8,128)(2,1)} %all-gather.5.cloned.1.call-done) | data formatting | bytes 8388608 | tf_op jit(solution)/shard_map/all_gather | solution.py:81
  119.3 7.3 %reshape.200 = bf16[512,4096]{1,0:T(8,128)(2,1)} reshape(bf16[64,4,2,4096]{3,2,1,0:T(2,128)(2,1)} %copy.94) | data formatting | bytes 8388608 | tf_op jit(solution)/shard_map/reshape | solution.py:87
  126.6 5.7 %fusion.8 = f32[512,384]{1,0:T(8,128)S(1)} fusion(bf16[512,4096]{1,0:T(8,128)(2,1)} %reshape.200, bf16[1,4096,384]{2,1,0:T(8,128)(2,1)} %param.15), kind=kOutput, calls=%fused_computation.13 | convolution fusion | flops 1610612736 | bytes 8126464 | tf_op jit(solution)/shard_map/dot_general | solution.py:94
  132.4 3.3 multiply_convert_fusion.1
  135.7 0.9 dot_general.47
  136.6 7.6 %fusion.4 = f32[64,4,2,4096]{3,0,2,1:T(8,128)} fusion(bf16[1,384,4096]{2,1,0:T(8,128)(2,1)} %param.17, bf16[64,4,2,384]{3,2,1,0:T(2,128)(2,1)} %dot_general.47), kind=kOutput, calls=%fused_computation.9 | convolution fusion | flops 1610612736 | bytes 11927552 | tf_op jit(solution)/shard_map/dot_general | solution.py:112
  144.2 0.0 reduce-scatter.5.cloned.1.call-update
  144.2 0.0 reduce-scatter.3.cloned.1.call-start
  144.3 0.6 copy-done.11
  144.9 1.0 fusion.30
  145.9 0.7 copy.83
  146.6 15.4 %all_to_all.27 = bf16[64,1,2]{2,1,0:T(2,128)(2,1)} all-to-all(bf16[64,1,2]{2,1,0:T(2,128)(2,1)} %copy.83), channel_id=1, replica_groups=mesh['roll'=4,'exp'=64] {'exp'}, dimensions={0} | all-to-all | bytes 512 | tf_op jit(solution)/shard_map/all_to_all | solution.py:78
  162.0 0.8 copy.84
  162.8 5.2 %all_gather.9 = bf16[64,4,2]{0,2,1:T(2,128)(2,1)S(1)} all-gather(bf16[64,1,2]{0,2,1:T(2,128)(2,1)S(1)} %copy.84), channel_id=1, replica_groups=mesh['roll'=4,'exp'=64] {'roll'}, dimensions={1}, use_global_device_ids=true | all-gather | bytes 1280 | tf_op jit(solution)/shard_map/all_gather | solution.py:83
  168.0 0.8 copy.86
  168.8 1.1 reshape.204
  169.8 0.0 all-gather.3.cloned.1.call-done
  169.8 8.5 %copy.90 = bf16[64,4,2,4096]{3,2,1,0:T(2,128)(2,1)} copy(bf16[64,4,2,4096]{3,0,2,1:T(8,128)(2,1)} %all-gather.3.cloned.1.call-done) | data formatting | bytes 8388608 | tf_op jit(solution)/shard_map/all_gather | solution.py:82
  178.4 7.4 %reshape.199 = bf16[512,4096]{1,0:T(8,128)(2,1)} reshape(bf16[64,4,2,4096]{3,2,1,0:T(2,128)(2,1)} %copy.90) | data formatting | bytes 8388608 | tf_op jit(solution)/shard_map/reshape | solution.py:88
  185.8 5.7 %fusion.17 = f32[512,384]{1,0:T(8,128)S(1)} fusion(bf16[512,4096]{1,0:T(8,128)(2,1)} %reshape.199, bf16[1,384,4096]{2,1,0:T(8,128)(2,1)} %param.17, f32[512]{0:T(512)S(1)} %reshape.204), kind=kOutput, calls=%fused_computation.24 | convolution fusion | flops 1610809344 | bytes 8128512 | tf_op jit(solution)/shard_map/dot_general | solution.py:98
  191.6 2.5 fusion.6
  194.1 5.7 %convolution_add_fusion = f32[512,4096]{1,0:T(8,128)} fusion(f32[512,4096]{1,0:T(8,128)S(1)} %fusion.6, bf16[1,4096,384]{2,1,0:T(8,128)(2,1)S(1)} %copy-done, f32[512,384]{1,0:T(8,128)S(1)} %fusion.17, f32[512,384]{1,0:T(8,128)S(1)} %copy-done.2), kind=kOutput, calls=%fused_computation | convolution fusion | flops 1613889536 | bytes 21495808 | tf_op jit(solution)/shard_map/dot_general | solution.py:106
  199.7 11.1 %reshape.201 = f32[64,4,2,4096]{3,2,1,0:T(2,128)} reshape(f32[512,4096]{1,0:T(8,128)} %convolution_add_fusion) | data formatting | bytes 16777216 | tf_op jit(solution)/shard_map/reshape | solution.py:107
  210.8 11.6 %copy.95 = f32[64,4,2,4096]{3,0,2,1:T(8,128)} copy(f32[64,4,2,4096]{3,2,1,0:T(2,128)} %reshape.201) | data formatting | bytes 16777216 | tf_op jit(solution)/shard_map/reshape | solution.py:107
  222.4 0.0 reduce-scatter.3.cloned.1.call-update
  222.4 21.5 %reduce-scatter.5.cloned.1.call-done = f32[64,1,2,4096]{3,0,2,1:T(8,128)} async-done(((f32[64,4,2,4096]{3,0,2,1:T(8,128)}), f32[64,1,2,4096]{3,0,2,1:T(8,128)}) %reduce-scatter.5.cloned.1.call-update) | async-done | bytes 2097168 | tf_op jit(solution)/shard_map/reduce_scatter | solution.py:115
  243.9 2.2 multiply_reduce_fusion
  246.1 0.7 copy.100
  246.8 11.0 %all-to-all-start.4 = ((bf16[64,1,2]{2,1,0:T(2,128)(2,1)}), bf16[64,1,2]{2,1,0:T(2,128)(2,1)}, u32[]{:S(2)}, u32[]{:S(2)}) async-start(bf16[64,1,2]{2,1,0:T(2,128)(2,1)} %copy.100), calls=%async_computation.6 | async-start | bytes 65536 | tf_op jit(solution)/shard_map/all_to_all | solution.py:123
  257.9 71.4 %reduce-scatter.3.cloned.1.call-done = f32[64,1,2,4096]{3,0,2,1:T(8,128)} async-done(((f32[64,4,2,4096]{3,0,2,1:T(8,128)}), f32[64,1,2,4096]{3,0,2,1:T(8,128)}) %reduce-scatter.3.cloned.1.call-update) | async-done | bytes 2097168 | tf_op jit(solution)/shard_map/reduce_scatter | solution.py:118
  329.2 1.7 convert_element_type.155
  331.0 2.1 copy.96
  333.1 10.8 %all-to-all-start.3 = ((bf16[64,1,2,4096]{3,2,1,0:T(2,128)(2,1)}), bf16[64,1,2,4096]{3,2,1,0:T(2,128)(2,1)}, u32[]{:S(2)}, u32[]{:S(2)}) async-start(bf16[64,1,2,4096]{3,2,1,0:T(2,128)(2,1)} %copy.96), calls=%async_computation.4 | async-start | bytes 2097152 | tf_op jit(solution)/shard_map/all_to_all | solution.py:120
  343.9 5.8 %fusion = bf16[1,384,4096]{2,1,0:T(8,128)(2,1)} fusion(bf16[512,4096]{1,0:T(8,128)(2,1)} %reshape.199, bf16[512,384]{1,0:T(8,128)(2,1)S(1)} %get-tuple-element.8, f32[512]{0:T(512)S(1)} %reshape.204), kind=kOutput, calls=%fused_computation.2 | convolution fusion | flops 1612775424 | bytes 7735296 | tf_op jit(solution)/shard_map/dot_general | solution.py:109
  349.6 0.8 copy.101
  350.5 0.9 fusion.28
  351.4 0.6 convert_element_type.161
  352.0 20.3 %all-to-all-done.3 = bf16[64,1,2,4096]{3,2,1,0:T(2,128)(2,1)} async-done(((bf16[64,1,2,4096]{3,2,1,0:T(2,128)(2,1)}), bf16[64,1,2,4096]{3,2,1,0:T(2,128)(2,1)}, u32[]{:S(2)}, u32[]{:S(2)}) %all-to-all-start.3) | async-done | bytes 1048608 | tf_op jit(solution)/shard_map/all_to_all | solution.py:120
  372.3 3.1 fusion.3
  (26 shorter events, 0.1 us)
Async XLA Ops:
  7.2 125.2 %copy-start = (bf16[1,4096,384]{2,1,0:T(8,128)(2,1)S(1)}, bf16[1,4096,384]{2,1,0:T(8,128)(2,1)}, u32[]{:S(2)}) copy-start(bf16[1,4096,384]{2,1,0:T(8,128)(2,1)} %param.16) | copy-start | bytes 9437188
  7.2 103.6 %all-gather.5.cloned.1.call-start = ((), (), s32[]{:S(2)}) async-start(), calls=%async_computation.8 | async-start | bytes 5242880 | tf_op jit(solution)/shard_map/all_gather | solution.py:81
  8.9 2.3 copy-start.6
  10.6 0.6 copy-start.7
  13.7 43.1 %copy-start.9 = (s32[1,4]{1,0:T(1,128)S(1)}, s32[1,4]{1,0:T(1,128)}, u32[]{:S(2)}) copy-start(s32[1,4]{1,0:T(1,128)} %param.14) | copy-start | bytes 52
  13.7 43.7 %copy-start.10 = (s32[1,4]{1,0:T(1,128)S(1)}, s32[1,4]{1,0:T(1,128)}, u32[]{:S(2)}) copy-start(s32[1,4]{1,0:T(1,128)} %param.13) | copy-start | bytes 52
  13.7 57.1 %copy-start.8 = (bf16[8,4096]{1,0:T(8,128)(2,1)S(1)}, bf16[8,4096]{1,0:T(8,128)(2,1)}, u32[]{:S(2)}) copy-start(bf16[8,4096]{1,0:T(8,128)(2,1)} %param.10) | copy-start | bytes 196612
  56.7 113.1 %all-gather.3.cloned.1.call-start = ((), (), s32[]{:S(2)}) async-start(), calls=%async_computation.7 | async-start | bytes 5242880 | tf_op jit(solution)/shard_map/all_gather | solution.py:82
  110.6 133.4 %reduce-scatter.5.cloned.1.call-start = ((), (), s32[]{:S(2)}) async-start(), calls=%async_computation.10 | async-start | bytes 10485760 | tf_op jit(solution)/shard_map/reduce_scatter | solution.py:115
  126.6 5.7 %copy-start.3 = (bf16[512,4096]{1,0:T(8,128)(2,1)S(1)}, bf16[512,4096]{1,0:T(8,128)(2,1)}, u32[]{:S(2)}) copy-start(bf16[512,4096]{1,0:T(8,128)(2,1)} %reshape.200) | copy-start | bytes 12582916
  132.4 3.3 copy-start.1
  144.2 0.7 copy-start.11
  144.2 185.0 %reduce-scatter.3.cloned.1.call-start = ((), (), s32[]{:S(2)}) async-start(), calls=%async_computation.9 | async-start | bytes 10485760 | tf_op jit(solution)/shard_map/reduce_scatter | solution.py:118
  185.8 5.8 %copy-start.2 = (f32[512,384]{1,0:T(8,128)S(1)}, f32[512,384]{1,0:T(8,128)}, u32[]{:S(2)}) copy-start(f32[512,384]{1,0:T(8,128)} %copy-done.1) | copy-start | bytes 2359300
  185.8 5.8 %copy-start.4 = (bf16[1,4096,384]{2,1,0:T(8,128)(2,1)S(1)}, bf16[1,4096,384]{2,1,0:T(8,128)(2,1)}, u32[]{:S(2)}) copy-start(bf16[1,4096,384]{2,1,0:T(8,128)(2,1)} %param.15) | copy-start | bytes 9437188
  185.8 5.8 %copy-start.5 = (f32[512,384]{1,0:T(8,128)S(1)}, f32[512,384]{1,0:T(8,128)}, u32[]{:S(2)}) copy-start(f32[512,384]{1,0:T(8,128)} %get-tuple-element.9) | copy-start | bytes 2359300
  246.8 86.3 %all-to-all-start.4 = ((bf16[64,1,2]{2,1,0:T(2,128)(2,1)}), bf16[64,1,2]{2,1,0:T(2,128)(2,1)}, u32[]{:S(2)}, u32[]{:S(2)}) async-start(bf16[64,1,2]{2,1,0:T(2,128)(2,1)} %copy.100), calls=%async_computation.6 | async-start | bytes 65536 | tf_op jit(solution)/shard_map/all_to_all | solution.py:123
  333.1 39.3 %all-to-all-start.3 = ((bf16[64,1,2,4096]{3,2,1,0:T(2,128)(2,1)}), bf16[64,1,2,4096]{3,2,1,0:T(2,128)(2,1)}, u32[]{:S(2)}, u32[]{:S(2)}) async-start(bf16[64,1,2,4096]{3,2,1,0:T(2,128)(2,1)} %copy.96), calls=%async_computation.4 | async-start | bytes 2097152 | tf_op jit(solution)/shard_map/all_to_all | solution.py:120
Sparse Core Ops, SparseCore 0:
  56.9 47.8 all-gather.4
  110.7 47.0 all-gather.2
  160.4 83.4 reduce-scatter.4
  246.4 82.8 reduce-scatter.2
where the time goes:
time: 389 us; the launch traced here: 382 us
  waiting for transfers between devices  113 us (29%)
  blocking collectives  108 us (28%)
  local copies, waits for them, and re-layouts  70.1 us (18%)
  matrix products  43 us (11%)
  starting transfers between devices  22.2 us (6%)
  between operations  17.5 us (4%)
  other arithmetic  8.24 us (2%)
    reduce_scatter x1, waiting for transfers between devices, on_device(): lax.psum_scatter(input_part, 'roll', scatter_dimension=1, tiled=True)  71.4 us
    all_to_all x1, blocking collectives, on_device(): lax.all_to_all(row_block, 'exp', split_axis=0, concat_axis=0, tiled=True)  41.5 us
    all_to_all x1, blocking collectives, on_device(): lax.all_to_all(grad_block, 'exp', split_axis=0, concat_axis=0, tiled=True)  36.6 us
    reshape x2, local copies, waits for them, and re-layouts, on_device(): input_part = input_part.reshape(n_source, n_block, cap_in, width)  22.7 us
    reduce_scatter x1, waiting for transfers between devices, on_device(): lax.psum_scatter(out_part, 'roll', scatter_dimension=1, tiled=True)  21.5 us
    all_to_all x1, waiting for transfers between devices, on_device(): lax.all_to_all(input_own.astype(jnp.bfloat16), 'exp', split_axis=0, conca...  20.3 us
    all_to_all x1, blocking collectives, on_device(): lax.all_to_all(prob_block, 'exp', split_axis=0, concat_axis=0, tiled=True)  15.4 us
    all_to_all x1, starting transfers between devices, on_device(): lax.all_to_all(prob_own.astype(jnp.bfloat16), 'exp', split_axis=0, concat...  11 us
  transfers between devices with their start and end apart: 6, of which 3 were waited for; matrix products, arithmetic and copies ran while one was open for 29% of the time, Pallas kernels for 0%

commit v1 on v0

v1 whole, which is shorter than its diff:
```python
import jax
import jax.numpy as jnp
from jax import lax
from jax.sharding import PartitionSpec as P

BF = jnp.bfloat16
F32 = jnp.float32
META = 128
CONTRACT_LAST = (((1,), (1,)), ((), ()))
CONTRACT_FIRST = (((0,), (0,)), ((), ()))


def silu_parts(pre_value):
    sigmoid_value = jax.nn.sigmoid(pre_value)
    return (pre_value * sigmoid_value, sigmoid_value * (1.0 + pre_value * (1.0 - sigmoid_value)))


def slot_layout(ids, experts, capacity):
    tok_count, top_count = ids.shape
    chosen = (ids[..., None] == jnp.arange(experts, dtype=jnp.int32)).astype(F32)
    per_token = jnp.sum(chosen, axis=1)
    before = jnp.cumsum(per_token, axis=0) - per_token
    layout = chosen[..., None] * (
        before[:, None, :, None] == jnp.arange(capacity, dtype=F32)
    ).astype(F32)
    return layout.reshape(tok_count, top_count, experts * capacity)


def ring(n_roll, step):
    return [(i, (i + step) % n_roll) for i in range(n_roll)]


def sum_over_roll(values):
    values = values + lax.ppermute(values, "roll", [(0, 1), (1, 0), (2, 3), (3, 2)])
    return values + lax.ppermute(values, "roll", [(0, 2), (2, 0), (1, 3), (3, 1)])


def gather_roll(rows):
    up, down = ring(4, 1), ring(4, -1)
    half = rows.shape[0] // 2
    from_left = lax.ppermute(rows, "roll", up)
    from_right = lax.ppermute(rows, "roll", down)
    far = jnp.concatenate(
        [
            lax.ppermute(from_left[:half], "roll", up),
            lax.ppermute(from_right[half:], "roll", down),
        ],
        axis=0,
    )
    return [rows, from_right, far, from_left]


def scatter_roll(parts):
    up, down = ring(4, 1), ring(4, -1)
    half = parts[0].shape[0] // 2
    far = parts[2].astype(BF)
    far_a = lax.ppermute(far[:half], "roll", up)
    far_b = lax.ppermute(far[half:], "roll", down)
    next_a = jnp.concatenate([parts[1][:half] + far_a.astype(F32), parts[1][half:]], axis=0)
    next_b = jnp.concatenate([parts[3][:half], parts[3][half:] + far_b.astype(F32)], axis=0)
    got_a = lax.ppermute(next_a.astype(BF), "roll", up)
    got_b = lax.ppermute(next_b.astype(BF), "roll", down)
    return parts[0] + got_a.astype(F32) + got_b.astype(F32)


def on_device(
    tokens,
    cotangent,
    router_probs,
    expert_ids,
    rewards,
    lengths,
    gate_weight,
    up_weight,
    down_weight,
):
    experts = lax.axis_size("exp")
    n_roll = lax.axis_size("roll")
    tok_count, width = tokens.shape
    top_count = expert_ids.shape[1]
    capacity = 2
    slots = experts * capacity
    w_gate, w_up, w_down = gate_weight[0], up_weight[0], down_weight[0]

    layout = slot_layout(expert_ids, experts, capacity)
    pick = jnp.sum(layout, axis=1).astype(BF)

    def pack(rows):
        return lax.dot_general(pick, rows, CONTRACT_FIRST, preferred_element_type=F32).astype(BF)

    def exchange(rows):
        return lax.all_to_all(rows, "exp", split_axis=0, concat_axis=0, tiled=True)

    own_rows = exchange(pack(tokens))
    all_rows = lax.all_gather(own_rows, "roll", axis=0, tiled=True)

    reward_f = rewards[0].astype(F32)
    length_f = lengths[0].astype(F32)
    sums = jnp.stack([jnp.sum(reward_f), jnp.sum(reward_f * reward_f), jnp.sum(length_f)])
    totals, squares, spans = sum_over_roll(sums)
    group_size = rewards.shape[1] * n_roll
    mean_reward = totals / group_size
    spread = jnp.sqrt(squares / group_size - mean_reward * mean_reward)
    advantage = (reward_f - mean_reward) / jnp.maximum(spread, 1.0)
    weights = advantage * (spans / group_size) / length_f
    token_weight = jnp.repeat(weights, tok_count // rewards.shape[1])
    scaled = (token_weight[:, None] * cotangent.astype(F32)).astype(BF)
    meta = jnp.concatenate(
        [
            router_probs,
            expert_ids.astype(BF),
            jnp.zeros((tok_count, META - 2 * top_count), BF),
        ],
        axis=1,
    )
    grad_own = exchange(pack(jnp.concatenate([scaled, meta], axis=1)))
    grad_pieces = gather_roll(grad_own)

    pre_gate = jnp.dot(all_rows, w_gate, preferred_element_type=F32)
    pre_up = jnp.dot(all_rows, w_up, preferred_element_type=F32)
    roll_index = lax.axis_index("roll")
    my_expert = lax.axis_index("exp").astype(F32)

    def piece_of(array, d):
        return lax.dynamic_slice_in_dim(
            array, lax.rem(roll_index + d, n_roll) * slots, slots, axis=0
        )

    parts, weighted_pieces = [None] * n_roll, [None] * n_roll
    for d in (0, 1, 3, 2):
        grads = grad_pieces[d][:, :width]
        info = grad_pieces[d][:, width:].astype(F32)
        prob = jnp.sum(
            jnp.where(
                info[:, top_count : 2 * top_count] == my_expert, info[:, :top_count], 0.0
            ),
            axis=1,
            keepdims=True,
        )
        gate_d, up_d = piece_of(pre_gate, d), piece_of(pre_up, d)
        activated, slope = silu_parts(gate_d)
        hidden = (activated * up_d).astype(BF)
        back_hidden = lax.dot_general(grads, w_down, CONTRACT_LAST, preferred_element_type=F32)
        hidden_grad = prob * back_hidden
        gate_grad = (hidden_grad * up_d * slope).astype(BF)
        up_grad = (hidden_grad * activated).astype(BF)
        input_part = lax.dot_general(
            gate_grad, w_gate, CONTRACT_LAST, preferred_element_type=F32
        ) + lax.dot_general(up_grad, w_up, CONTRACT_LAST, preferred_element_type=F32)
        prob_part = jnp.sum(hidden.astype(F32) * back_hidden, axis=1, keepdims=True)
        weighted_pieces[d] = (prob * hidden.astype(F32)).astype(BF)
        parts[d] = jnp.concatenate([input_part, split_value(prob_part)], axis=1)
    own_sum = scatter_roll(parts)
    prob_sum = own_sum[:, width : width + 1] + own_sum[:, width + 1 : width + 2]
    returned = exchange(
        jnp.concatenate([own_sum[:, :width], split_value(prob_sum)], axis=1).astype(BF)
    )
    grad_tokens = lax.dot_general(
        pick, returned[:, :width], (((1,), (0,)), ((), ())), preferred_element_type=F32
    ).astype(BF)
    slot_prob = returned[:, width].astype(F32) + returned[:, width + 1].astype(F32)
    grad_probs = jnp.sum(layout * slot_prob, axis=2).astype(BF)

    down_grad = lax.dot_general(
        jnp.concatenate(weighted_pieces, axis=0),
        jnp.concatenate([piece[:, :width] for piece in grad_pieces], axis=0),
        CONTRACT_FIRST,
        preferred_element_type=F32,
    )
    return (grad_tokens, grad_probs, down_grad.astype(BF)[None])


def split_value(value):
    high = lax.reduce_precision(value, 8, 7)
    rest = (value - high).astype(BF).astype(F32)
    return jnp.concatenate(
        [high, rest, jnp.zeros((value.shape[0], META - 2), F32)], axis=1
    )


def solution(mesh):
    in_specs = (
        P(("roll", "exp"), None),
        P(("roll", "exp"), None),
        P(("roll", "exp"), None),
        P(("roll", "exp"), None),
        P("exp", "roll"),
        P("exp", "roll"),
        P("exp", None, "roll"),
        P("exp", None, "roll"),
        P("exp", "roll", None),
    )
    out_specs = (P(("roll", "exp"), None), P(("roll", "exp"), None), P("exp", "roll", None))
    return jax.shard_map(
        on_device, mesh=mesh, in_specs=in_specs, out_specs=out_specs, check_vma=False
    )
```

time: 389 us -> 320 us (0.82); the launches traced: 382 us -> 318 us
  blocking collectives: 108 us -> 0 us
  starting transfers between devices: 22.2 us -> 48.4 us
  other arithmetic: 8.24 us -> 26.1 us
  matrix products: 43 us -> 54 us
  local copies, waits for them, and re-layouts: 70.1 us -> 60.2 us
    all_to_all x3 -> x0, blocking collectives: 93.4 us -> none  [the longest x1 41.5 us: on_device(): lax.all_to_all(row_block, 'exp', split_axis=0, concat_axis=0, tiled=True)]
    reduce_scatter x2 -> x0, waiting for transfers between devices: 92.9 us -> none  [the longest x1 71.4 us: on_device(): lax.psum_scatter(input_part, 'roll', scatter_dimension=1, tiled=True)]
    ppermute x0 -> x10, waiting for transfers between devices: none -> 56.4 us  [the longest x1 39.6 us: gather_roll(): from_left = lax.ppermute(rows, 'roll', up)]
    reshape x4 -> x0, local copies, waits for them, and re-layouts: 37.4 us -> none  [the longest x2 22.7 us: on_device(): input_part = input_part.reshape(n_source, n_block, cap_in, width)]
    all_to_all x2 -> x3, waiting for transfers between devices: 20.3 us -> 54.8 us  [exchange(): return lax.all_to_all(rows, 'exp', split_axis=0, concat_axis=0, tiled=True)]
    concatenate x0 -> x9, local copies, waits for them, and re-layouts: none -> 23.4 us  [the longest x4 13.8 us: on_device(): parts[d] = jnp.concatenate([input_part, split_value(prob_part)], axis=1)]
    all_gather x2 -> x0, local copies, waits for them, and re-layouts: 17 us -> none  [the longest x1 8.52 us: on_device(): lax.all_gather(sent_rows, 'roll', axis=1, tiled=True)]
    ppermute x0 -> x10, starting transfers between devices: none -> 16.1 us  [the longest x1 3.41 us: scatter_roll(): far_b = lax.ppermute(far[half:], 'roll', down)]
  transfers between devices with their start and end apart: 6 -> 14, of which waited for: 3 -> 10; matrix products, arithmetic and copies ran while one was open for 29% -> 22% of each run, Pallas kernels for 0% -> 0%
where the time goes in v1:
time: 320 us; the launch traced here: 318 us
  waiting for transfers between devices  111 us (35%)
  local copies, waits for them, and re-layouts  60.2 us (19%)
  matrix products  54 us (17%)
  starting transfers between devices  48.4 us (15%)
  other arithmetic  26.1 us (8%)
  between operations  17.9 us (6%)
    all_to_all x3, waiting for transfers between devices, exchange(): return lax.all_to_all(rows, 'exp', split_axis=0, concat_axis=0, tiled=True)  54.8 us
    ppermute x1, waiting for transfers between devices, gather_roll(): from_left = lax.ppermute(rows, 'roll', up)  39.6 us
    all_to_all x3, starting transfers between devices, exchange(): return lax.all_to_all(rows, 'exp', split_axis=0, concat_axis=0, tiled=True)  32.2 us
    dot_general x4, matrix products, on_device(): lax.dot_general(up_grad, w_up, CONTRACT_LAST, preferred_element_type=F32)  17.8 us
    concatenate x4, local copies, waits for them, and re-layouts, on_device(): parts[d] = jnp.concatenate([input_part, split_value(prob_part)], axis=1)  13.8 us
    all_to_all x5, local copies, waits for them, and re-layouts, exchange(): return lax.all_to_all(rows, 'exp', split_axis=0, concat_axis=0, tiled=True)  11.7 us
    dot_general x4, matrix products, on_device(): lax.dot_general(grads, w_down, CONTRACT_LAST, preferred_element_type=F32)  10.5 us
    ppermute x1, waiting for transfers between devices, scatter_roll(): got_a = lax.ppermute(next_a.astype(BF), 'roll', up)  10.4 us
  transfers between devices with their start and end apart: 14, of which 10 were waited for; matrix products, arithmetic and copies ran while one was open for 22% of the time, Pallas kernels for 0%

profile of v1, /device:TPU:1, one launch (start us, length us, event | category | flops | bytes accessed | tf_op | source)
XLA Modules:
  0.0 317.8 jit_solution(6683591996789110427)
XLA Ops:
  9.7 2.2 convolution_convert_fusion.2
  11.9 2.6 all_to_all.25
  14.5 13.2 %all-to-all-start.1 = ((bf16[64,2,4096]{2,1,0:T(2,128)(2,1)}), bf16[64,2,4096]{2,1,0:T(2,128)(2,1)}, u32[]{:S(2)}, u32[]{:S(2)}) async-start(bf16[64,2,4096]{2,1,0:T(2,128)(2,1)} %all_to_all.25), calls=%async_computation.1 | async-start | bytes 2097152 | tf_op jit(solution)/shard_map/all_to_all | solution.py:92
  28.9 2.0 pad_maximum_fusion.2
  30.9 1.3 collective-permute-start
  32.3 1.5 collective-permute-done
  33.8 2.0 fusion.117
  35.8 2.9 collective-permute-start.1
  38.7 1.4 collective-permute-done.1
  40.1 2.0 fusion.118
  46.4 1.4 convolution_convert_fusion
  47.7 2.3 all_to_all.22
  50.0 6.2 %all-to-all-done.1 = bf16[64,2,4096]{2,1,0:T(2,128)(2,1)} async-done(((bf16[64,2,4096]{2,1,0:T(2,128)(2,1)}), bf16[64,2,4096]{2,1,0:T(2,128)(2,1)}, u32[]{:S(2)}, u32[]{:S(2)}) %all-to-all-start.1) | async-done | bytes 1048608 | tf_op jit(solution)/shard_map/all_to_all | solution.py:92
  56.2 6.4 %all-to-all-start = ((bf16[64,2,4224]{2,1,0:T(2,128)(2,1)}), bf16[64,2,4224]{2,1,0:T(2,128)(2,1)}, u32[]{:S(2)}, u32[]{:S(2)}) async-start(bf16[64,2,4224]{2,1,0:T(2,128)(2,1)} %all_to_all.22), calls=%async_computation | async-start | bytes 2162688 | tf_op jit(solution)/shard_map/all_to_all | solution.py:92
  62.6 2.2 all_to_all.27
  64.9 26.9 %all-to-all-done = bf16[64,2,4224]{2,1,0:T(2,128)(2,1)} async-done(((bf16[64,2,4224]{2,1,0:T(2,128)(2,1)}), bf16[64,2,4224]{2,1,0:T(2,128)(2,1)}, u32[]{:S(2)}, u32[]{:S(2)}) %all-to-all-start) | async-done | bytes 1081376 | tf_op jit(solution)/shard_map/all_to_all | solution.py:92
  91.7 2.3 all_to_all.24
  94.0 1.3 collective-permute-start.3
  95.3 1.4 collective-permute-start.2
  97.7 3.5 %fusion.31 = f32[128,384]{1,0:T(8,128)S(1)} fusion(bf16[1,384,4096]{2,1,0:T(8,128)(2,1)} %param.17, bf16[128,4224]{1,0:T(8,128)(2,1)} %all_to_all.24), kind=kOutput, calls=%fused_computation.39 | convolution fusion | flops 402653184 | bytes 4390912 | tf_op jit(solution)/shard_map/dot_general | solution.py:143
  101.2 39.6 %collective-permute-done.3 = bf16[128,4224]{1,0:T(8,128)(2,1)} collective-permute-done((bf16[128,4224]{1,0:T(8,128)(2,1)}, bf16[128,4224]{1,0:T(8,128)(2,1)}, u32[]{:S(2)}, u32[]{:S(2)}) %collective-permute-start.3) | collective-permute-done | bytes 1081376 | tf_op jit(solution)/shard_map/ppermute | solution.py:41
  143.1 2.9 collective-permute-start.5
  147.5 3.0 fusion.25
  151.4 3.0 fusion.29
  154.4 2.1 collective-permute-done.4
  159.0 4.7 %fusion.17 = f32[512,384]{1,0:T(8,128)S(1)} fusion(bf16[512,4096]{1,0:T(8,128)(2,1)} %all-gather.2.cloned.1.call-done, bf16[1,4096,384]{2,1,0:T(8,128)(2,1)S(1)} %copy-done), kind=kOutput, calls=%fused_computation.25 | convolution fusion | flops 1610612736 | bytes 8126464 | tf_op jit(solution)/shard_map/dot_general | solution.py:119
  163.7 2.4 fusion.23
  166.1 2.5 fusion.13
  170.9 2.5 fusion.11
  173.3 2.5 fusion.9
  177.2 1.3 copy.81
  178.5 1.4 copy.80
  179.9 1.4 copy.85
  181.3 1.3 copy.77
  182.6 1.4 copy.84
  184.0 1.4 copy.76
  185.4 4.8 %fusion.1 = bf16[128,4096]{1,0:T(8,128)(2,1)} fusion(f32[128,4096]{1,0:T(8,128)} %fusion.11, bf16[1,4096,384]{2,1,0:T(8,128)(2,1)} %param.16, f32[128,384]{1,0:T(8,128)S(1)} %fusion.27, f32[128]{0:T(128)} %fusion.70, f32[512,384]{1,0:T(8,128)} %copy-done.5, s32[]{:T(128)S(6)} %select_n.34), kind=kOutput, calls=%fused_computation.7 | convolution fusion | flops 404045824 | bytes 6685188 | tf_op jit(solution)/shard_map/dot_general | solution.py:149
  190.8 3.1 concatenate.50
  193.9 2.5 fusion.108
  196.4 3.4 %collective-permute-start.8 = (bf16[64,4224]{1,0:T(8,128)(2,1)}, bf16[64,4224]{1,0:T(8,128)(2,1)}, u32[]{:S(2)}, u32[]{:S(2)}) collective-permute-start(bf16[64,4224]{1,0:T(8,128)(2,1)} %get-tuple-element.22), channel_id=1, source_target_pairs={{0,192},{64,0},{128,64},{192,128},{1,193},{65,1},{129,65},{193,129... | collective-permute-start | bytes 1622024 | tf_op jit(solution)/shard_map/ppermute | solution.py:58
  199.8 4.5 %convolution_add_fusion.2 = f32[128,4096]{1,0:T(8,128)} fusion(f32[128,4096]{1,0:T(8,128)S(1)} %copy-done.4, bf16[1,4096,384]{2,1,0:T(8,128)(2,1)} %param.16, f32[128,384]{1,0:T(8,128)S(1)} %copy-done.13, f32[128]{0:T(128)S(1)} %copy-done.27, f32[512,384]{1,0:T(8,128)} %copy-done.5, s32[]{:T(128)S(6)} %select_n.32), kind=kOutput, calls=%fused_computation.5 | convolution fusion | flops 403521536 | bytes 7733764 | tf_op jit(solution)/shard_map/dot_general | solution.py:149
  204.9 3.6 %concatenate.48 = f32[128,4224]{1,0:T(8,128)} concatenate(f32[128,4096]{1,0:T(8,128)} %convolution_add_fusion.2, f32[128,1]{1,0:T(8,128)} %copy.76, f32[128,1]{1,0:T(8,128)} %copy.77, f32[128,126]{1,0:T(8,128)} %broadcast.48), dimensions={1} | concatenate | bytes 4325376 | tf_op jit(solution)/shard_map/concatenate | solution.py:152
  208.5 2.1 slice.218
  210.7 5.0 %convolution_add_fusion = f32[128,4096]{1,0:T(8,128)} fusion(f32[128,4096]{1,0:T(8,128)} %fusion.9, bf16[1,4096,384]{2,1,0:T(8,128)(2,1)} %param.16, f32[128,384]{1,0:T(8,128)S(1)} %copy-done.11, f32[128]{0:T(128)S(1)} %fusion.69, f32[512,384]{1,0:T(8,128)} %copy-done.5, s32[]{:T(128)S(6)} %select_n.36), kind=kOutput, calls=%fused_computation.3 | convolution fusion | flops 403521536 | bytes 7733764 | tf_op jit(solution)/shard_map/dot_general | solution.py:149
  215.7 3.6 %concatenate.52 = f32[128,4224]{1,0:T(8,128)} concatenate(f32[128,4096]{1,0:T(8,128)} %convolution_add_fusion, f32[128,1]{1,0:T(8,128)} %copy.84, f32[128,1]{1,0:T(8,128)} %copy.85, f32[128,126]{1,0:T(8,128)} %broadcast.48), dimensions={1} | concatenate | bytes 4325376 | tf_op jit(solution)/shard_map/concatenate | solution.py:152
  219.2 1.4 slice.217
  220.6 1.6 fusion.34
  225.6 2.7 collective-permute-start.9
  228.5 2.3 fusion.15
  230.9 3.4 %convolution_add_fusion.3 = f32[128,4096]{1,0:T(8,128)} fusion(f32[128,4096]{1,0:T(8,128)S(1)} %fusion.15, bf16[1,4096,384]{2,1,0:T(8,128)(2,1)S(1)} %copy-done.3, f32[128,384]{1,0:T(8,128)S(1)} %fusion.31, f32[128]{0:T(128)S(1)} %fusion.72, f32[512,384]{1,0:T(8,128)} %copy-done.5, s32[]{:T(128)S(6)} %select_n.30), kind=kOutput, calls=%fused_computation.6 | convolution fusion | flops 403521536 | bytes 7733764 | tf_op jit(solution)/shard_map/dot_general | solution.py:149
  234.3 3.5 %concatenate.47 = f32[128,4224]{1,0:T(8,128)} concatenate(f32[128,4096]{1,0:T(8,128)} %convolution_add_fusion.3, f32[128,1]{1,0:T(8,128)S(1)} %copy.72, f32[128,1]{1,0:T(8,128)S(1)} %copy.73, f32[128,126]{1,0:T(8,128)S(1)} %copy-done.15), dimensions={1} | concatenate | bytes 4325376 | tf_op jit(solution)/shard_map/concatenate | solution.py:152
  237.8 10.4 %collective-permute-done.7 = bf16[128,4224]{1,0:T(8,128)(2,1)} collective-permute-done((bf16[128,4224]{1,0:T(8,128)(2,1)}, bf16[128,4224]{1,0:T(8,128)(2,1)}, u32[]{:S(2)}, u32[]{:S(2)}) %collective-permute-start.7) | collective-permute-done | bytes 1081376 | tf_op jit(solution)/shard_map/ppermute | solution.py:61
  248.2 1.2 collective-permute-done.9
  249.4 2.5 convert_add_fusion
  253.1 2.5 concatenate.54
  255.7 7.0 %concatenate.58 = bf16[64,2,4224]{2,1,0:T(2,128)(2,1)} concatenate(bf16[64,2,4096]{2,1,0:T(2,128)(2,1)} %concatenate.54, bf16[64,2,1]{2,1,0:T(2,128)(2,1)S(1)} %bitcast.85, bf16[64,2,1]{2,1,0:T(2,128)(2,1)S(1)} %bitcast.84, bf16[64,2,126]{2,1,0:T(2,128)(2,1)S(1)} %concatenate.57), dimensions={2} | concatenate | bytes 2162688 | tf_op jit(solution)/shard_map/concatenate | solution.py:156
  262.7 12.7 %all-to-all-start.2 = ((bf16[64,2,4224]{2,1,0:T(2,128)(2,1)}), bf16[64,2,4224]{2,1,0:T(2,128)(2,1)}, u32[]{:S(2)}, u32[]{:S(2)}) async-start(bf16[64,2,4224]{2,1,0:T(2,128)(2,1)} %concatenate.58), calls=%async_computation.2 | async-start | bytes 2162688 | tf_op jit(solution)/shard_map/all_to_all | solution.py:92
  275.4 1.3 slice.130
  276.7 1.4 slice.147
  278.2 1.4 slice.134
  279.7 3.2 %fusion = bf16[1,384,4096]{2,1,0:T(8,128)(2,1)} fusion(bf16[128,4096]{1,0:T(8,128)(2,1)S(1)} %slice.147, bf16[128,4096]{1,0:T(8,128)(2,1)S(1)} %slice.141, bf16[128,4096]{1,0:T(8,128)(2,1)S(1)} %slice.134, bf16[128,4096]{1,0:T(8,128)(2,1)S(1)} %slice.130, bf16[128,384]{1,0:T(8,128)(2,1)S(1)} %copy-done.23, bf16[128,384]{1,0:T(8,128)(2,1)S(1)} %copy-done.22, ...), kind=kOutput, calls=%fused_computation.2 | convolution fusion | flops 1630535680 | bytes 7733248 | tf_op jit(solution)/shard_map/dot_general | solution.py:164
  282.9 21.7 %all-to-all-done.2 = bf16[64,2,4224]{2,1,0:T(2,128)(2,1)} async-done(((bf16[64,2,4224]{2,1,0:T(2,128)(2,1)}), bf16[64,2,4224]{2,1,0:T(2,128)(2,1)}, u32[]{:S(2)}, u32[]{:S(2)}) %all-to-all-start.2) | async-done | bytes 1081376 | tf_op jit(solution)/shard_map/all_to_all | solution.py:92
  304.6 2.3 all_to_all.29
  307.9 2.2 convolution_convert_fusion.3
  (130 shorter events, 24.4 us)
Async XLA Ops:
  7.2 151.8 %copy-start = (bf16[1,4096,384]{2,1,0:T(8,128)(2,1)S(1)}, bf16[1,4096,384]{2,1,0:T(8,128)(2,1)}, u32[]{:S(2)}) copy-start(bf16[1,4096,384]{2,1,0:T(8,128)(2,1)} %param.15) | copy-start | bytes 9437188
  8.9 0.6 copy-start.18
  9.6 36.7 %copy-start.16 = (bf16[8,64,2]{0,2,1:T(2,128)(2,1)}, bf16[8,64,2]{0,2,1:T(2,128)(2,1)S(1)}, u32[]{:S(2)}) copy-start(bf16[8,64,2]{0,2,1:T(2,128)(2,1)S(1)} %copy.69) | copy-start | bytes 6148
  11.9 15.8 %copy-start.32 = (s32[1,4]{1,0:T(1,128)S(1)}, s32[1,4]{1,0:T(1,128)}, u32[]{:S(2)}) copy-start(s32[1,4]{1,0:T(1,128)} %param.13) | copy-start | bytes 52
  11.9 16.4 %copy-start.31 = (s32[1,4]{1,0:T(1,128)S(1)}, s32[1,4]{1,0:T(1,128)}, u32[]{:S(2)}) copy-start(s32[1,4]{1,0:T(1,128)} %param.14) | copy-start | bytes 52
  11.9 20.4 %copy-start.25 = (s32[8,8]{1,0:T(8,128)S(1)}, s32[8,8]{1,0:T(8,128)}, u32[]{:S(2)}) copy-start(s32[8,8]{1,0:T(8,128)} %param.12) | copy-start | bytes 772
  11.9 34.3 %copy-start.24 = (bf16[8,4096]{1,0:T(8,128)(2,1)S(1)}, bf16[8,4096]{1,0:T(8,128)(2,1)}, u32[]{:S(2)}) copy-start(bf16[8,4096]{1,0:T(8,128)(2,1)} %param.10) | copy-start | bytes 196612
  11.9 34.4 %copy-start.29 = (bf16[8,8]{1,0:T(8,128)(2,1)S(1)}, bf16[8,8]{1,0:T(8,128)(2,1)}, u32[]{:S(2)}) copy-start(bf16[8,8]{1,0:T(8,128)(2,1)} %param.11) | copy-start | bytes 388
  14.5 41.7 %all-to-all-start.1 = ((bf16[64,2,4096]{2,1,0:T(2,128)(2,1)}), bf16[64,2,4096]{2,1,0:T(2,128)(2,1)}, u32[]{:S(2)}, u32[]{:S(2)}) async-start(bf16[64,2,4096]{2,1,0:T(2,128)(2,1)} %all_to_all.25), calls=%async_computation.1 | async-start | bytes 2097152 | tf_op jit(solution)/shard_map/all_to_all | solution.py:92
  30.9 2.8 collective-permute-start
  35.8 4.3 %collective-permute-start.1 = (f32[3]{0:T(128)S(1)}, f32[3]{0:T(128)S(1)}, u32[]{:S(2)}, u32[]{:S(2)}) collective-permute-start(f32[3]{0:T(128)S(1)} %fusion.117), channel_id=1, source_target_pairs={{0,128},{128,0},{64,192},{192,64},{1,129},{129,1},{65,193},{193,65... | collective-permute-start | bytes 44 | tf_op jit(solution)/shard_map/ppermute | solution.py:35
  56.2 35.6 %all-to-all-start = ((bf16[64,2,4224]{2,1,0:T(2,128)(2,1)}), bf16[64,2,4224]{2,1,0:T(2,128)(2,1)}, u32[]{:S(2)}, u32[]{:S(2)}) async-start(bf16[64,2,4224]{2,1,0:T(2,128)(2,1)} %all_to_all.22), calls=%async_computation | async-start | bytes 2162688 | tf_op jit(solution)/shard_map/all_to_all | solution.py:92
  62.5 96.4 %all-gather.2.cloned.1.call-start = ((), (), s32[]{:S(2)}) async-start(), calls=%async_computation.3 | async-start | bytes 5242880 | tf_op jit(solution)/shard_map/all_gather | solution.py:95
  94.0 46.8 %collective-permute-start.3 = (bf16[128,4224]{1,0:T(8,128)(2,1)}, bf16[128,4224]{1,0:T(8,128)(2,1)}, u32[]{:S(2)}, u32[]{:S(2)}) collective-permute-start(bf16[128,4224]{1,0:T(8,128)(2,1)} %all_to_all.24), channel_id=1, source_target_pairs={{0,64},{64,128},{128,192},{192,0},{1,65},{65,129},{129,193},{193,1... | collective-permute-start | bytes 3244040 | tf_op jit(solution)/shard_map/ppermute | solution.py:41
  95.3 46.7 %collective-permute-start.2 = (bf16[128,4224]{1,0:T(8,128)(2,1)}, bf16[128,4224]{1,0:T(8,128)(2,1)}, u32[]{:S(2)}, u32[]{:S(2)}) collective-permute-start(bf16[128,4224]{1,0:T(8,128)(2,1)} %all_to_all.24), channel_id=1, source_target_pairs={{0,192},{64,0},{128,64},{192,128},{1,193},{65,1},{129,65},{193,129... | collective-permute-start | bytes 3244040 | tf_op jit(solution)/shard_map/ppermute | solution.py:42
  97.7 49.8 %copy-start.1 = (bf16[1,384,4096]{2,1,0:T(8,128)(2,1)S(1)}, bf16[1,384,4096]{2,1,0:T(8,128)(2,1)}, u32[]{:S(2)}) copy-start(bf16[1,384,4096]{2,1,0:T(8,128)(2,1)} %param.17) | copy-start | bytes 9437188
  141.9 14.6 %collective-permute-start.4 = (bf16[64,4224]{1,0:T(8,128)(2,1)S(1)}, bf16[64,4224]{1,0:T(8,128)(2,1)S(1)}, u32[]{:S(2)}, u32[]{:S(2)}) collective-permute-start(bf16[64,4224]{1,0:T(8,128)(2,1)S(1)} %slice.136), channel_id=1, source_target_pairs={{0,64},{64,128},{128,192},{192,0},{1,65},{65,129},{129,193},{193,1... | collective-permute-start | bytes 1622024 | tf_op jit(solution)/shard_map/ppermute | solution.py:45
  143.1 13.7 %collective-permute-start.5 = (bf16[64,4224]{1,0:T(8,128)(2,1)S(1)}, bf16[64,4224]{1,0:T(8,128)(2,1)S(1)}, u32[]{:S(2)}, u32[]{:S(2)}) collective-permute-start(bf16[64,4224]{1,0:T(8,128)(2,1)S(1)} %slice.137), channel_id=1, source_target_pairs={{0,192},{64,0},{128,64},{192,128},{1,193},{65,1},{129,65},{193,129... | collective-permute-start | bytes 1622024 | tf_op jit(solution)/shard_map/ppermute | solution.py:46
  156.8 1.1 copy-start.7
  159.0 4.7 %copy-start.2 = (bf16[1,4096,384]{2,1,0:T(8,128)(2,1)S(1)}, bf16[1,4096,384]{2,1,0:T(8,128)(2,1)}, u32[]{:S(2)}) copy-start(bf16[1,4096,384]{2,1,0:T(8,128)(2,1)} %param.16) | copy-start | bytes 9437188
  159.0 4.7 %copy-start.33 = (bf16[512,4096]{1,0:T(8,128)(2,1)S(1)}, bf16[512,4096]{1,0:T(8,128)(2,1)}, u32[]{:S(2)}) copy-start(bf16[512,4096]{1,0:T(8,128)(2,1)} %all-gather.2.cloned.1.call-done) | copy-start | bytes 12582916
  163.7 9.6 %copy-start.5 = (f32[512,384]{1,0:T(8,128)}, f32[512,384]{1,0:T(8,128)S(1)}, u32[]{:S(2)}) copy-start(f32[512,384]{1,0:T(8,128)S(1)} %fusion.17) | copy-start | bytes 2359300
  163.7 2.4 copy-start.12
  163.7 2.4 copy-start.26
  166.1 7.2 %copy-start.9 = (f32[512,384]{1,0:T(8,128)}, f32[512,384]{1,0:T(8,128)S(1)}, u32[]{:S(2)}) copy-start(f32[512,384]{1,0:T(8,128)S(1)} %fusion.23) | copy-start | bytes 2359300
  166.1 2.5 copy-start.28
  170.9 2.5 copy-start.10
  190.8 9.0 %copy-start.13 = (f32[128,384]{1,0:T(8,128)S(1)}, f32[128,384]{1,0:T(8,128)}, u32[]{:S(2)}) copy-start(f32[128,384]{1,0:T(8,128)} %fusion.29) | copy-start | bytes 589828
  193.9 5.9 %copy-start.4 = (f32[128,4096]{1,0:T(8,128)S(1)}, f32[128,4096]{1,0:T(8,128)}, u32[]{:S(2)}) copy-start(f32[128,4096]{1,0:T(8,128)} %fusion.13) | copy-start | bytes 6291460
  193.9 5.9 %copy-start.27 = (f32[128]{0:T(128)S(1)}, f32[128]{0:T(128)}, u32[]{:S(2)}) copy-start(f32[128]{0:T(128)} %fusion.71) | copy-start | bytes 1540
  196.4 24.2 %collective-permute-start.6 = (bf16[64,4224]{1,0:T(8,128)(2,1)}, bf16[64,4224]{1,0:T(8,128)(2,1)}, u32[]{:S(2)}, u32[]{:S(2)}) collective-permute-start(bf16[64,4224]{1,0:T(8,128)(2,1)} %get-tuple-element.21), channel_id=1, source_target_pairs={{0,64},{64,128},{128,192},{192,0},{1,65},{65,129},{129,193},{193,1... | collective-permute-start | bytes 1622024 | tf_op jit(solution)/shard_map/ppermute | solution.py:57
  196.4 26.9 %collective-permute-start.8 = (bf16[64,4224]{1,0:T(8,128)(2,1)}, bf16[64,4224]{1,0:T(8,128)(2,1)}, u32[]{:S(2)}, u32[]{:S(2)}) collective-permute-start(bf16[64,4224]{1,0:T(8,128)(2,1)} %get-tuple-element.22), channel_id=1, source_target_pairs={{0,192},{64,0},{128,64},{192,128},{1,193},{65,1},{129,65},{193,129... | collective-permute-start | bytes 1622024 | tf_op jit(solution)/shard_map/ppermute | solution.py:58
  204.9 5.8 %copy-start.11 = (f32[128,384]{1,0:T(8,128)S(1)}, f32[128,384]{1,0:T(8,128)}, u32[]{:S(2)}) copy-start(f32[128,384]{1,0:T(8,128)} %fusion.25) | copy-start | bytes 589828
  219.2 3.0 copy-start.14
  220.6 2.7 copy-start.6
  223.3 4.9 %copy-start.30 = (f32[128]{0:T(128)S(1)}, f32[128]{0:T(128)}, u32[]{:S(2)}) copy-start(f32[128]{0:T(128)} %get-tuple-element.34) | copy-start | bytes 1540
  223.3 24.9 %collective-permute-start.7 = (bf16[128,4224]{1,0:T(8,128)(2,1)}, bf16[128,4224]{1,0:T(8,128)(2,1)}, u32[]{:S(2)}, u32[]{:S(2)}) collective-permute-start(bf16[128,4224]{1,0:T(8,128)(2,1)} %pad_maximum_fusion), channel_id=1, source_target_pairs={{0,64},{64,128},{128,192},{192,0},{1,65},{65,129},{129,193},{193,1... | collective-permute-start | bytes 3244040 | tf_op jit(solution)/shard_map/ppermute | solution.py:61
  225.6 23.8 %collective-permute-start.9 = (bf16[128,4224]{1,0:T(8,128)(2,1)}, bf16[128,4224]{1,0:T(8,128)(2,1)}, u32[]{:S(2)}, u32[]{:S(2)}) collective-permute-start(bf16[128,4224]{1,0:T(8,128)(2,1)} %pad_maximum_fusion.1), channel_id=1, source_target_pairs={{0,192},{64,0},{128,64},{192,128},{1,193},{65,1},{129,65},{193,129... | collective-permute-start | bytes 3244040 | tf_op jit(solution)/shard_map/ppermute | solution.py:62
  228.5 2.4 copy-start.3
  230.8 3.4 %copy-start.15 = (f32[128,126]{1,0:T(8,128)S(1)}, f32[128,126]{1,0:T(8,128)}, u32[]{:S(2)}) copy-start(f32[128,126]{1,0:T(8,128)} %broadcast.48) | copy-start | bytes 193540
  262.7 41.9 %all-to-all-start.2 = ((bf16[64,2,4224]{2,1,0:T(2,128)(2,1)}), bf16[64,2,4224]{2,1,0:T(2,128)(2,1)}, u32[]{:S(2)}, u32[]{:S(2)}) async-start(bf16[64,2,4224]{2,1,0:T(2,128)(2,1)} %concatenate.58), calls=%async_computation.2 | async-start | bytes 2162688 | tf_op jit(solution)/shard_map/all_to_all | solution.py:92
  276.7 2.8 copy-start.8
  278.1 1.5 copy-start.20
  278.1 1.5 copy-start.21
  278.2 1.5 copy-start.22
  278.2 1.5 copy-start.23
  282.9 25.0 %copy-start.17 = (bf16[8,64,2]{0,2,1:T(2,128)(2,1)S(1)}, bf16[8,64,2]{0,2,1:T(2,128)(2,1)}, u32[]{:S(2)}) copy-start(bf16[8,64,2]{0,2,1:T(2,128)(2,1)} %copy-done.16) | copy-start | bytes 6148
  282.9 27.4 %copy-start.19 = (f32[8,8,64]{2,1,0:T(8,128)S(1)}, f32[8,8,64]{2,1,0:T(8,128)}, u32[]{:S(2)}) copy-start(f32[8,8,64]{2,1,0:T(8,128)} %copy-done.18) | copy-start | bytes 49156
Sparse Core Ops, SparseCore 0:
  65.8 71.0 all-gather.1

commit v2 on v1

v2 whole, which is shorter than its diff:
```python
import jax
import jax.numpy as jnp
from jax import lax
from jax.experimental import pallas as pl
from jax.experimental.pallas import tpu as pltpu
from jax.sharding import PartitionSpec as P

BF = jnp.bfloat16
F32 = jnp.float32
META = 128
N_Y = 4
CAP = 2
OUTER_BLOCK = 1024
VMEM_LIMIT = 48 * 1024 * 1024
CONTRACT_LAST = (((1,), (1,)), ((), ()))
CONTRACT_FIRST = (((0,), (0,)), ((), ()))
PLAIN = (((1,), (0,)), ((), ()))


def dot(a, b, dims=PLAIN):
    return lax.dot_general(a, b, dims, preferred_element_type=F32)


def outer_kernel(count, *refs):
    weighted = jnp.concatenate([ref[...] for ref in refs[:count]], axis=0)
    rows = jnp.concatenate([ref[...] for ref in refs[count : 2 * count]], axis=0)
    refs[-1][...] = dot(weighted, rows, CONTRACT_FIRST).astype(BF)


def outer(weighted, pieces, width):
    hidden = weighted[0].shape[1]
    return pl.pallas_call(
        lambda *refs: outer_kernel(len(pieces), *refs),
        grid=(width // OUTER_BLOCK,),
        in_specs=[pl.BlockSpec(array.shape, lambda i: (0, 0)) for array in weighted]
        + [pl.BlockSpec((piece.shape[0], OUTER_BLOCK), lambda i: (0, i)) for piece in pieces],
        out_specs=pl.BlockSpec((hidden, OUTER_BLOCK), lambda i: (0, i)),
        out_shape=jax.ShapeDtypeStruct((hidden, width), BF),
        compiler_params=pltpu.CompilerParams(vmem_limit_bytes=VMEM_LIMIT),
        name="outer",
    )(*weighted, *pieces)


def slot_layout(ids, experts):
    tok_count, top_count = ids.shape
    chosen = (ids[..., None] == jnp.arange(experts, dtype=jnp.int32)).astype(F32)
    per_token = jnp.sum(chosen, axis=1)
    before = jnp.cumsum(per_token, axis=0) - per_token
    layout = chosen[:, :, None, :] * (
        before[:, None, None, :] == jnp.arange(CAP, dtype=F32)[:, None]
    ).astype(F32)
    return layout.reshape(tok_count, top_count, CAP * experts)


def silu_parts(pre_value):
    sigmoid_value = jax.nn.sigmoid(pre_value)
    return (pre_value * sigmoid_value, sigmoid_value * (1.0 + pre_value * (1.0 - sigmoid_value)))


def split_value(value):
    high = lax.reduce_precision(value, 8, 7)
    return high, value - high


def move(rows, step):
    return lax.ppermute(rows, "roll", [(i, (i + step) % N_Y) for i in range(N_Y)])


def gather_near(rows):
    return move(rows, -1), move(rows, 1)


def gather_far(right, left):
    half = left.shape[0] // 2
    return jnp.concatenate([move(left[:half], 1), move(right[half:], -1)], axis=0)


def on_device(
    tokens,
    cotangent,
    router_probs,
    expert_ids,
    rewards,
    lengths,
    gate_weight,
    up_weight,
    down_weight,
):
    experts = lax.axis_size("exp")
    tok_count, width = tokens.shape
    top = expert_ids.shape[1]
    w_gate, w_up, w_down = gate_weight[0], up_weight[0], down_weight[0]
    my_expert = lax.axis_index("exp").astype(F32)

    layout = slot_layout(expert_ids, experts)
    pick = jnp.sum(layout, axis=1).astype(BF)

    def pack(rows):
        return dot(pick, rows, CONTRACT_FIRST).astype(BF)

    def exchange(rows):
        rows = rows.reshape(CAP, experts, rows.shape[1])
        rows = lax.all_to_all(rows, "exp", split_axis=1, concat_axis=1, tiled=True)
        return rows.reshape(CAP * experts, rows.shape[2])

    meta = [
        router_probs,
        expert_ids.astype(BF),
        jnp.zeros((tok_count, META - 2 * top), BF),
    ]
    tok_own = exchange(pack(jnp.concatenate([tokens] + meta, axis=1)))

    both = jnp.concatenate([rewards, lengths], axis=1).astype(F32)
    four = jnp.concatenate([both] + [move(both, step) for step in (1, 2, 3)], axis=0)
    members = rewards.shape[1]
    group_size = members * N_Y
    totals = jnp.sum(four[:, :members])
    squares = jnp.sum(four[:, :members] * four[:, :members])
    spans = jnp.sum(four[:, members:])
    mean_reward = totals / group_size
    spread = jnp.sqrt(squares / group_size - mean_reward * mean_reward)
    advantage = (both[0, :members] - mean_reward) / jnp.maximum(spread, 1.0)
    weights = advantage * (spans / group_size) / both[0, members:]
    token_weight = jnp.repeat(weights, tok_count // members)
    scaled = (token_weight[:, None] * cotangent.astype(F32)).astype(BF)
    tok_right, tok_left = gather_near(tok_own)
    tok_far = gather_far(tok_right, tok_left)
    grad_own = exchange(pack(scaled))
    grad_own, tok_right, tok_left = lax.optimization_barrier((grad_own, tok_right, tok_left))
    grad_right, grad_left = gather_near(grad_own)
    grad_far = gather_far(grad_right, grad_left)
    tok_own, tok_right, tok_left, tok_far = lax.optimization_barrier(
        (tok_own, tok_right, tok_left, tok_far)
    )

    lane = jnp.arange(META)

    def hidden_rows(rows, grads):
        info = rows[:, width:].astype(F32)
        prob = jnp.sum(
            jnp.where(info[:, top : 2 * top] == my_expert, info[:, :top], 0.0),
            axis=1,
            keepdims=True,
        )
        pre_gate, pre_up = dot(rows[:, :width], w_gate), dot(rows[:, :width], w_up)
        activated, slope = silu_parts(pre_gate)
        hidden = (activated * pre_up).astype(BF)
        back_hidden = dot(grads, w_down, CONTRACT_LAST)
        hidden_grad = prob * back_hidden
        gate_grad = (hidden_grad * pre_up * slope).astype(BF)
        up_grad = (hidden_grad * activated).astype(BF)
        high, rest = split_value(
            jnp.sum(hidden.astype(F32) * back_hidden, axis=1, keepdims=True)
        )
        tail = jnp.where(lane == 0, high, jnp.where(lane == 1, rest, 0.0)).astype(BF)
        return (gate_grad, up_grad, tail), (prob * hidden.astype(F32)).astype(BF)

    def input_part(gate_grad, up_grad, tail):
        part = dot(gate_grad, w_gate, CONTRACT_LAST) + dot(up_grad, w_up, CONTRACT_LAST)
        return jnp.concatenate([part.astype(BF), tail], axis=1)

    from_own, weighted_own = hidden_rows(tok_own, grad_own)
    from_right, weighted_right = hidden_rows(tok_right, grad_right)
    from_left, weighted_left = hidden_rows(tok_left, grad_left)
    from_right, from_left, grad_far = lax.optimization_barrier((from_right, from_left, grad_far))
    part_right, part_left = input_part(*from_right), input_part(*from_left)
    grad_far, part_right, part_left = lax.optimization_barrier((grad_far, part_right, part_left))
    from_far, weighted_far = hidden_rows(tok_far, grad_far)
    part_far = input_part(*from_far)
    part_own = input_part(*from_own)
    total = part_own.astype(F32)
    for rows in (move(part_right, 1), move(part_left, -1), move(part_far, 2)):
        total = total + rows.astype(F32)
    high, rest = split_value(total[:, width : width + 1] + total[:, width + 1 : width + 2])
    column = jnp.arange(width + META)
    returned = exchange(
        jnp.where(column == width, high, jnp.where(column == width + 1, rest, total)).astype(BF)
    )
    grad_tokens = dot(pick, returned[:, :width]).astype(BF)
    slot_prob = returned[:, width].astype(F32) + returned[:, width + 1].astype(F32)
    grad_probs = jnp.sum(layout * slot_prob, axis=2).astype(BF)
    down_grad = outer(
        [weighted_own, weighted_right, weighted_left, weighted_far],
        [grad_own, grad_right, grad_left, grad_far],
        width,
    )
    return (grad_tokens, grad_probs, down_grad[None])


def solution(mesh):
    in_specs = (
        P(("roll", "exp"), None),
        P(("roll", "exp"), None),
        P(("roll", "exp"), None),
        P(("roll", "exp"), None),
        P("exp", "roll"),
        P("exp", "roll"),
        P("exp", None, "roll"),
        P("exp", None, "roll"),
        P("exp", "roll", None),
    )
    out_specs = (P(("roll", "exp"), None), P(("roll", "exp"), None), P("exp", "roll", None))
    return jax.shard_map(
        on_device, mesh=mesh, in_specs=in_specs, out_specs=out_specs, check_vma=False
    )
```

time: 320 us -> 243 us (0.76)
  local copies, waits for them, and re-layouts: 60.2 us -> 21.2 us
  matrix products: 54 us -> 21.7 us
  waiting for transfers between devices: 111 us -> 132 us
  other arithmetic: 26.1 us -> 8.51 us
  between operations: 17.9 us -> 4.42 us
  Pallas kernels: 0 us -> 3.82 us
    ppermute x10 -> x14, waiting for transfers between devices: 56.4 us -> 96.1 us  [move(): lax.ppermute(rows, 'roll', [(i, (i + step) % N_Y) for i in range(N_Y)])]
    dot_general x18 -> x23, matrix products: 54 us -> 21.7 us  [dot(): return lax.dot_general(a, b, dims, preferred_element_type=F32)]
    concatenate x9 -> x1, local copies, waits for them, and re-layouts: 23.4 us -> 0.93 us  [on_device(): tok_own = exchange(pack(jnp.concatenate([tokens] + meta, axis=1)))]
    all_to_all x3, waiting for transfers between devices: 54.8 us -> 36.1 us  [exchange(): rows = lax.all_to_all(rows, 'exp', split_axis=1, concat_axis=1, tiled=True)]
    slice x10 -> x4, local copies, waits for them, and re-layouts: 13.4 us -> 1.87 us  [the longest x2 0.94 us: gather_far(): left[:half]]
    all_to_all x5 -> x3, local copies, waits for them, and re-layouts: 11.7 us -> 4.65 us  [exchange(): rows = lax.all_to_all(rows, 'exp', split_axis=1, concat_axis=1, tiled=True)]
    reshape x0 -> x3, local copies, waits for them, and re-layouts: none -> 6.32 us  [exchange(): rows = rows.reshape(CAP, experts, rows.shape[1])]
    unnamed x69 -> x46, local copies, waits for them, and re-layouts: 0.91 us -> 7.09 us
  transfers between devices with their start and end apart: 14 -> 17, of which waited for: 10 -> 12; matrix products, arithmetic and copies ran while one was open for 22% -> 10% of each run, Pallas kernels for 0% -> 2%
where the time goes in v2:
time: 243 us; the launch traced here: 242 us
  waiting for transfers between devices  132 us (54%)
  starting transfers between devices  50.1 us (21%)
  matrix products  21.7 us (9%)
  local copies, waits for them, and re-layouts  21.2 us (9%)
  other arithmetic  8.51 us (4%)
  between operations  4.42 us (2%)
  Pallas kernels  3.82 us (2%)
    ppermute x14, waiting for transfers between devices, move(): lax.ppermute(rows, 'roll', [(i, (i + step) % N_Y) for i in range(N_Y)])  96.1 us
    all_to_all x3, waiting for transfers between devices, exchange(): rows = lax.all_to_all(rows, 'exp', split_axis=1, concat_axis=1, tiled=True)  36.1 us
    all_to_all x3, starting transfers between devices, exchange(): rows = lax.all_to_all(rows, 'exp', split_axis=1, concat_axis=1, tiled=True)  30.6 us
    dot_general x23, matrix products, dot(): return lax.dot_general(a, b, dims, preferred_element_type=F32)  21.7 us
    ppermute x14, starting transfers between devices, move(): lax.ppermute(rows, 'roll', [(i, (i + step) % N_Y) for i in range(N_Y)])  19.5 us
    unnamed x46, local copies, waits for them, and re-layouts  7.09 us
    reshape x3, local copies, waits for them, and re-layouts, exchange(): rows = rows.reshape(CAP, experts, rows.shape[1])  6.32 us
  transfers between devices with their start and end apart: 17, of which 12 were waited for; matrix products, arithmetic and copies ran while one was open for 10% of the time, Pallas kernels for 2%

profile of v2, /device:TPU:1, one launch (start us, length us, event | category | flops | bytes accessed | tf_op | source)
XLA Modules:
  0.0 241.9 jit_solution(8616658886936407631)
XLA Ops:
  0.6 0.9 fusion.77
  1.6 0.8 fusion.76
  2.4 0.7 convert_element_type.191
  3.2 0.9 concatenate.35
  4.7 2.1 copy.24
  6.8 13.2 %all-to-all-start = ((bf16[2,64,4224]{2,0,1:T(2,128)(2,1)}), bf16[2,64,4224]{2,0,1:T(2,128)(2,1)}, u32[]{:S(2)}, u32[]{:S(2)}) async-start(bf16[2,64,4224]{2,0,1:T(2,128)(2,1)} %copy.24), calls=%async_computation | async-start | bytes 2162688 | tf_op jit(solution)/shard_map/all_to_all | solution.py:103
  20.1 1.3 collective-permute-start
  21.4 2.6 %collective-permute-start.1 = (f32[1,8]{1,0:T(1,128)S(1)}, f32[1,8]{1,0:T(1,128)S(1)}, u32[]{:S(2)}, u32[]{:S(2)}) collective-permute-start(f32[1,8]{1,0:T(1,128)S(1)} %add_convert_fusion), channel_id=1, source_target_pairs={{0,128},{64,192},{128,0},{192,64},{1,129},{65,193},{129,1},{193,65... | collective-permute-start | bytes 104 | tf_op jit(solution)/shard_map/ppermute | solution.py:66
  24.0 1.1 collective-permute-start.2
  25.7 1.1 collective-permute-done.2
  26.8 0.7 slice_reduce_fusion.1
  31.5 2.1 copy.26
  33.6 15.6 %all-to-all-done = bf16[2,64,4224]{2,0,1:T(2,128)(2,1)} async-done(((bf16[2,64,4224]{2,0,1:T(2,128)(2,1)}), bf16[2,64,4224]{2,0,1:T(2,128)(2,1)}, u32[]{:S(2)}, u32[]{:S(2)}) %all-to-all-start) | async-done | bytes 1081376 | tf_op jit(solution)/shard_map/all_to_all | solution.py:103
  49.2 6.4 %all-to-all-start.1 = ((bf16[2,64,4096]{2,0,1:T(2,128)(2,1)}), bf16[2,64,4096]{2,0,1:T(2,128)(2,1)}, u32[]{:S(2)}, u32[]{:S(2)}) async-start(bf16[2,64,4096]{2,0,1:T(2,128)(2,1)} %copy.26), calls=%async_computation.1 | async-start | bytes 2097152 | tf_op jit(solution)/shard_map/all_to_all | solution.py:103
  55.5 1.3 copy.25
  56.9 1.4 collective-permute-start.4
  58.3 2.3 collective-permute-start.3
  60.6 22.7 %collective-permute-done.4 = bf16[128,4224]{1,0:T(8,128)(2,1)S(1)} collective-permute-done((bf16[128,4224]{1,0:T(8,128)(2,1)S(1)}, bf16[128,4224]{1,0:T(8,128)(2,1)S(1)}, u32[]{:S(2)}, u32[]{:S(2)}) %collective-permute-start.4) | collective-permute-done | bytes 1081376 | tf_op jit(solution)/shard_map/ppermute | solution.py:66
  83.3 0.9 slice.122
  84.5 0.9 slice.123
  85.7 2.4 %collective-permute-start.6 = (bf16[64,4224]{1,0:T(8,128)(2,1)}, bf16[64,4224]{1,0:T(8,128)(2,1)}, u32[]{:S(2)}, u32[]{:S(2)}) collective-permute-start(bf16[64,4224]{1,0:T(8,128)(2,1)} %slice.123), channel_id=1, source_target_pairs={{0,192},{64,0},{128,64},{192,128},{1,193},{65,1},{129,65},{193,129... | collective-permute-start | bytes 1622024 | tf_op jit(solution)/shard_map/ppermute | solution.py:66
  88.6 2.0 copy.27
  91.0 1.3 collective-permute-start.8
  92.3 6.0 %collective-permute-done.5 = bf16[64,4224]{1,0:T(8,128)(2,1)} collective-permute-done((bf16[64,4224]{1,0:T(8,128)(2,1)}, bf16[64,4224]{1,0:T(8,128)(2,1)}, u32[]{:S(2)}, u32[]{:S(2)}) %collective-permute-start.5) | collective-permute-done | bytes 540704 | tf_op jit(solution)/shard_map/ppermute | solution.py:66
  98.5 1.3 pad_maximum_fusion
  99.8 0.7 fusion.14
  101.4 0.8 fusion.18
  102.4 0.8 fusion.50
  103.2 1.1 copy-done.10
  104.3 1.2 fusion.49
  105.7 0.7 fusion.12
  106.4 0.7 fusion.6
  107.2 0.8 fusion.56
  107.9 12.9 %collective-permute-done.7.refs_5_ = bf16[128,4096]{1,0:T(8,128)(2,1)S(1)} collective-permute-done((bf16[128,4096]{1,0:T(8,128)(2,1)S(1)}, bf16[128,4096]{1,0:T(8,128)(2,1)S(1)}, u32[]{:S(2)}, u32[]{:S(2)}) %collective-permute-start.7) | collective-permute-done | bytes 1048608 | tf_op jit(solution)/shard_map/ppermute | solution.py:66
  120.9 3.5 %collective-permute-start.10 = (bf16[64,4096]{1,0:T(8,128)(2,1)S(1)}, bf16[64,4096]{1,0:T(8,128)(2,1)S(1)}, u32[]{:S(2)}, u32[]{:S(2)}) collective-permute-start(bf16[64,4096]{1,0:T(8,128)(2,1)S(1)} %slice.131), channel_id=1, source_target_pairs={{0,192},{64,0},{128,64},{192,128},{1,193},{65,1},{129,65},{193,129... | collective-permute-start | bytes 1572872 | tf_op jit(solution)/shard_map/ppermute | solution.py:66
  124.7 1.1 fusion.36
  125.9 0.8 fusion.52
  126.8 1.1 fusion.34
  127.9 0.8 fusion.54
  129.1 4.1 %collective-permute-done.10 = bf16[64,4096]{1,0:T(8,128)(2,1)S(1)} collective-permute-done((bf16[64,4096]{1,0:T(8,128)(2,1)S(1)}, bf16[64,4096]{1,0:T(8,128)(2,1)S(1)}, u32[]{:S(2)}, u32[]{:S(2)}) %collective-permute-start.10) | collective-permute-done | bytes 524320 | tf_op jit(solution)/shard_map/ppermute | solution.py:66
  133.2 3.5 %collective-permute-done.9 = bf16[64,4096]{1,0:T(8,128)(2,1)S(1)} collective-permute-done((bf16[64,4096]{1,0:T(8,128)(2,1)S(1)}, bf16[64,4096]{1,0:T(8,128)(2,1)S(1)}, u32[]{:S(2)}, u32[]{:S(2)}) %collective-permute-start.9) | collective-permute-done | bytes 524320 | tf_op jit(solution)/shard_map/ppermute | solution.py:66
  136.7 1.1 fusion.8
  137.9 1.1 fusion.10
  139.0 1.1 fusion.2
  140.2 1.1 fusion.1
  141.5 1.2 fusion.55
  142.6 1.1 fusion.4
  143.8 1.2 fusion.3
  145.7 2.2 collective-permute-start.12
  148.0 1.2 fusion.16
  149.2 1.2 fusion
  150.3 18.2 %collective-permute-done.13 = bf16[128,4224]{1,0:T(8,128)(2,1)S(1)} collective-permute-done((bf16[128,4224]{1,0:T(8,128)(2,1)S(1)}, bf16[128,4224]{1,0:T(8,128)(2,1)S(1)}, u32[]{:S(2)}, u32[]{:S(2)}) %collective-permute-start.13) | collective-permute-done | bytes 1081376 | tf_op jit(solution)/shard_map/ppermute | solution.py:66
  168.5 26.7 %collective-permute-done.11 = bf16[128,4224]{1,0:T(8,128)(2,1)S(1)} collective-permute-done((bf16[128,4224]{1,0:T(8,128)(2,1)S(1)}, bf16[128,4224]{1,0:T(8,128)(2,1)S(1)}, u32[]{:S(2)}, u32[]{:S(2)}) %collective-permute-start.11) | collective-permute-done | bytes 1081376 | tf_op jit(solution)/shard_map/ppermute | solution.py:66
  196.3 2.2 copy.28
  198.4 11.1 %all-to-all-start.2 = ((bf16[2,64,4224]{2,0,1:T(2,128)(2,1)}), bf16[2,64,4224]{2,0,1:T(2,128)(2,1)}, u32[]{:S(2)}, u32[]{:S(2)}) async-start(bf16[2,64,4224]{2,0,1:T(2,128)(2,1)} %copy.28), calls=%async_computation.2 | async-start | bytes 2162688 | tf_op jit(solution)/shard_map/all_to_all | solution.py:103
  209.5 1.2 copy-done.2
  210.7 1.2 copy-done.4
  212.0 1.2 copy-done.6
  213.2 1.2 copy-done.8
  214.4 3.8 %outer.1 = bf16[384,4096]{1,0:T(8,128)(2,1)} custom-call(bf16[128,384]{1,0:T(8,128)(2,1)S(1)} %get-tuple-element.48.refs_0_, bf16[128,384]{1,0:T(8,128)(2,1)S(1)} %get-tuple-element.46.refs_1_, bf16[128,384]{1,0:T(8,128)(2,1)S(1)} %get-tuple-element.44.refs_2_, bf16[128,384]{1,0:T(8,128)(2,1)S(1)} %get-tuple-element.42.refs_3_, ...), custom_call_target="tpu_custom_call" | custom-call | tf_op jit(solution)/shard_map/outer/pallas_call | solution.py:32
  218.2 20.5 %all-to-all-done.2 = bf16[2,64,4224]{2,0,1:T(2,128)(2,1)} async-done(((bf16[2,64,4224]{2,0,1:T(2,128)(2,1)}), bf16[2,64,4224]{2,0,1:T(2,128)(2,1)}, u32[]{:S(2)}, u32[]{:S(2)}) %all-to-all-start.2) | async-done | bytes 1081376 | tf_op jit(solution)/shard_map/all_to_all | solution.py:103
  238.7 1.3 copy.29
  240.0 0.9 convolution_convert_fusion.2
  241.2 0.7 fusion.67
  (93 shorter events, 8.1 us)
Async XLA Ops:
  0.6 101.7 %copy-start = (bf16[1,4096,384]{2,1,0:T(8,128)(2,1)S(1)}, bf16[1,4096,384]{2,1,0:T(8,128)(2,1)}, u32[]{:S(2)}) copy-start(bf16[1,4096,384]{2,1,0:T(8,128)(2,1)} %param.16) | copy-start | bytes 9437188
  2.4 4.4 %copy-start.17 = (f32[8,8,64]{2,1,0:T(8,128)}, f32[8,8,64]{2,1,0:T(8,128)S(1)}, u32[]{:S(2)}) copy-start(f32[8,8,64]{2,1,0:T(8,128)S(1)} %fusion.76) | copy-start | bytes 49156
  4.7 15.3 %copy-start.21 = (s32[1,4]{1,0:T(1,128)S(1)}, s32[1,4]{1,0:T(1,128)}, u32[]{:S(2)}) copy-start(s32[1,4]{1,0:T(1,128)} %param.14) | copy-start | bytes 52
  4.7 15.3 %copy-start.22 = (s32[1,4]{1,0:T(1,128)S(1)}, s32[1,4]{1,0:T(1,128)}, u32[]{:S(2)}) copy-start(s32[1,4]{1,0:T(1,128)} %param.13) | copy-start | bytes 52
  4.7 26.3 %copy-start.19 = (bf16[8,4096]{1,0:T(8,128)(2,1)S(1)}, bf16[8,4096]{1,0:T(8,128)(2,1)}, u32[]{:S(2)}) copy-start(bf16[8,4096]{1,0:T(8,128)(2,1)} %param.10) | copy-start | bytes 196612
  6.8 42.4 %all-to-all-start = ((bf16[2,64,4224]{2,0,1:T(2,128)(2,1)}), bf16[2,64,4224]{2,0,1:T(2,128)(2,1)}, u32[]{:S(2)}, u32[]{:S(2)}) async-start(bf16[2,64,4224]{2,0,1:T(2,128)(2,1)} %copy.24), calls=%async_computation | async-start | bytes 2162688 | tf_op jit(solution)/shard_map/all_to_all | solution.py:103
  20.1 5.0 %collective-permute-start = (f32[1,8]{1,0:T(1,128)S(1)}, f32[1,8]{1,0:T(1,128)S(1)}, u32[]{:S(2)}, u32[]{:S(2)}) collective-permute-start(f32[1,8]{1,0:T(1,128)S(1)} %add_convert_fusion), channel_id=1, source_target_pairs={{0,64},{64,128},{128,192},{192,0},{1,65},{65,129},{129,193},{193,1... | collective-permute-start | bytes 104 | tf_op jit(solution)/shard_map/ppermute | solution.py:66
  21.4 4.3 %collective-permute-start.1 = (f32[1,8]{1,0:T(1,128)S(1)}, f32[1,8]{1,0:T(1,128)S(1)}, u32[]{:S(2)}, u32[]{:S(2)}) collective-permute-start(f32[1,8]{1,0:T(1,128)S(1)} %add_convert_fusion), channel_id=1, source_target_pairs={{0,128},{64,192},{128,0},{192,64},{1,129},{65,193},{129,1},{193,65... | collective-permute-start | bytes 104 | tf_op jit(solution)/shard_map/ppermute | solution.py:66
  24.0 2.8 %collective-permute-start.2 = (f32[1,8]{1,0:T(1,128)S(1)}, f32[1,8]{1,0:T(1,128)S(1)}, u32[]{:S(2)}, u32[]{:S(2)}) collective-permute-start(f32[1,8]{1,0:T(1,128)S(1)} %add_convert_fusion), channel_id=1, source_target_pairs={{0,192},{64,0},{128,64},{192,128},{1,193},{65,1},{129,65},{193,129... | collective-permute-start | bytes 104 | tf_op jit(solution)/shard_map/ppermute | solution.py:66
  49.2 39.5 %all-to-all-start.1 = ((bf16[2,64,4096]{2,0,1:T(2,128)(2,1)}), bf16[2,64,4096]{2,0,1:T(2,128)(2,1)}, u32[]{:S(2)}, u32[]{:S(2)}) async-start(bf16[2,64,4096]{2,0,1:T(2,128)(2,1)} %copy.26), calls=%async_computation.1 | async-start | bytes 2097152 | tf_op jit(solution)/shard_map/all_to_all | solution.py:103
  56.9 1.4 copy-start.11
  56.9 26.4 %collective-permute-start.4 = (bf16[128,4224]{1,0:T(8,128)(2,1)S(1)}, bf16[128,4224]{1,0:T(8,128)(2,1)S(1)}, u32[]{:S(2)}, u32[]{:S(2)}) collective-permute-start(bf16[128,4224]{1,0:T(8,128)(2,1)S(1)} %bitcast.84), channel_id=1, source_target_pairs={{0,64},{64,128},{128,192},{192,0},{1,65},{65,129},{129,193},{193,1... | collective-permute-start | bytes 3244040 | tf_op jit(solution)/shard_map/ppermute | solution.py:66
  58.3 26.0 %collective-permute-start.3 = (bf16[128,4224]{1,0:T(8,128)(2,1)S(1)}, bf16[128,4224]{1,0:T(8,128)(2,1)S(1)}, u32[]{:S(2)}, u32[]{:S(2)}) collective-permute-start(bf16[128,4224]{1,0:T(8,128)(2,1)S(1)} %bitcast.85), channel_id=1, source_target_pairs={{0,192},{64,0},{128,64},{192,128},{1,193},{65,1},{129,65},{193,129... | collective-permute-start | bytes 3244040 | tf_op jit(solution)/shard_map/ppermute | solution.py:66
  83.3 1.2 copy-start.13
  84.2 14.1 %collective-permute-start.5 = (bf16[64,4224]{1,0:T(8,128)(2,1)}, bf16[64,4224]{1,0:T(8,128)(2,1)}, u32[]{:S(2)}, u32[]{:S(2)}) collective-permute-start(bf16[64,4224]{1,0:T(8,128)(2,1)} %slice.122), channel_id=1, source_target_pairs={{0,64},{64,128},{128,192},{192,0},{1,65},{65,129},{129,193},{193,1... | collective-permute-start | bytes 1622024 | tf_op jit(solution)/shard_map/ppermute | solution.py:66
  84.5 1.2 copy-start.15
  85.7 12.8 %collective-permute-start.6 = (bf16[64,4224]{1,0:T(8,128)(2,1)}, bf16[64,4224]{1,0:T(8,128)(2,1)}, u32[]{:S(2)}, u32[]{:S(2)}) collective-permute-start(bf16[64,4224]{1,0:T(8,128)(2,1)} %slice.123), channel_id=1, source_target_pairs={{0,192},{64,0},{128,64},{192,128},{1,193},{65,1},{129,65},{193,129... | collective-permute-start | bytes 1622024 | tf_op jit(solution)/shard_map/ppermute | solution.py:66
  88.6 11.2 %copy-start.16 = (bf16[128,4224]{1,0:T(8,128)(2,1)S(1)}, bf16[128,4224]{1,0:T(8,128)(2,1)}, u32[]{:S(2)}) copy-start(bf16[128,4224]{1,0:T(8,128)(2,1)} %copy-done.15) | copy-start | bytes 3244036
  88.6 11.2 %copy-start.9 = (bf16[1,4096,384]{2,1,0:T(8,128)(2,1)S(1)}, bf16[1,4096,384]{2,1,0:T(8,128)(2,1)}, u32[]{:S(2)}) copy-start(bf16[1,4096,384]{2,1,0:T(8,128)(2,1)} %param.15) | copy-start | bytes 9437188
  90.6 12.6 %copy-start.1 = (bf16[2,64,4096]{2,1,0:T(8,128)(2,1)}, bf16[2,64,4096]{2,1,0:T(8,128)(2,1)S(1)}, u32[]{:S(2)}) copy-start(bf16[2,64,4096]{2,1,0:T(8,128)(2,1)S(1)} %copy.27) | copy-start | bytes 3145732
  90.6 30.3 %collective-permute-start.7 = (bf16[128,4096]{1,0:T(8,128)(2,1)S(1)}, bf16[128,4096]{1,0:T(8,128)(2,1)S(1)}, u32[]{:S(2)}, u32[]{:S(2)}) collective-permute-start(bf16[128,4096]{1,0:T(8,128)(2,1)S(1)} %bitcast.76), channel_id=1, source_target_pairs={{0,192},{64,0},{128,64},{192,128},{1,193},{65,1},{129,65},{193,129... | collective-permute-start | bytes 3145736 | tf_op jit(solution)/shard_map/ppermute | solution.py:66
  91.0 33.4 %collective-permute-start.8 = (bf16[128,4096]{1,0:T(8,128)(2,1)S(1)}, bf16[128,4096]{1,0:T(8,128)(2,1)S(1)}, u32[]{:S(2)}, u32[]{:S(2)}) collective-permute-start(bf16[128,4096]{1,0:T(8,128)(2,1)S(1)} %bitcast.77), channel_id=1, source_target_pairs={{0,64},{64,128},{128,192},{192,0},{1,65},{65,129},{129,193},{193,1... | collective-permute-start | bytes 3145736 | tf_op jit(solution)/shard_map/ppermute | solution.py:66
  99.8 1.2 copy-start.14
  99.8 1.6 copy-start.12
  102.4 1.9 copy-start.10
  120.8 5.0 %copy-start.5 = (bf16[128,4096]{1,0:T(8,128)(2,1)}, bf16[128,4096]{1,0:T(8,128)(2,1)S(1)}, u32[]{:S(2)}) copy-start(bf16[128,4096]{1,0:T(8,128)(2,1)S(1)} %collective-permute-done.7.refs_5_) | copy-start | bytes 3145732
  120.9 12.3 %collective-permute-start.10 = (bf16[64,4096]{1,0:T(8,128)(2,1)S(1)}, bf16[64,4096]{1,0:T(8,128)(2,1)S(1)}, u32[]{:S(2)}, u32[]{:S(2)}) collective-permute-start(bf16[64,4096]{1,0:T(8,128)(2,1)S(1)} %slice.131), channel_id=1, source_target_pairs={{0,192},{64,0},{128,64},{192,128},{1,193},{65,1},{129,65},{193,129... | collective-permute-start | bytes 1572872 | tf_op jit(solution)/shard_map/ppermute | solution.py:66
  124.4 2.4 copy-start.7
  124.4 12.2 %collective-permute-start.9 = (bf16[64,4096]{1,0:T(8,128)(2,1)S(1)}, bf16[64,4096]{1,0:T(8,128)(2,1)S(1)}, u32[]{:S(2)}, u32[]{:S(2)}) collective-permute-start(bf16[64,4096]{1,0:T(8,128)(2,1)S(1)} %slice.130), channel_id=1, source_target_pairs={{0,64},{64,128},{128,192},{192,0},{1,65},{65,129},{129,193},{193,1... | collective-permute-start | bytes 1572872 | tf_op jit(solution)/shard_map/ppermute | solution.py:66
  127.9 0.9 copy-start.20
  136.7 4.7 %copy-start.3 = (bf16[128,4096]{1,0:T(8,128)(2,1)}, bf16[128,4096]{1,0:T(8,128)(2,1)S(1)}, u32[]{:S(2)}) copy-start(bf16[128,4096]{1,0:T(8,128)(2,1)S(1)} %pad_maximum_fusion.4.refs_7_) | copy-start | bytes 3145732
  145.1 23.4 %collective-permute-start.13 = (bf16[128,4224]{1,0:T(8,128)(2,1)S(1)}, bf16[128,4224]{1,0:T(8,128)(2,1)S(1)}, u32[]{:S(2)}, u32[]{:S(2)}) collective-permute-start(bf16[128,4224]{1,0:T(8,128)(2,1)S(1)} %pad_maximum_fusion.3), channel_id=1, source_target_pairs={{0,128},{64,192},{128,0},{192,64},{1,129},{65,193},{129,1},{193,65... | collective-permute-start | bytes 3244040 | tf_op jit(solution)/shard_map/ppermute | solution.py:66
  145.2 50.0 %collective-permute-start.11 = (bf16[128,4224]{1,0:T(8,128)(2,1)S(1)}, bf16[128,4224]{1,0:T(8,128)(2,1)S(1)}, u32[]{:S(2)}, u32[]{:S(2)}) collective-permute-start(bf16[128,4224]{1,0:T(8,128)(2,1)S(1)} %pad_maximum_fusion.1), channel_id=1, source_target_pairs={{0,64},{64,128},{128,192},{192,0},{1,65},{65,129},{129,193},{193,1... | collective-permute-start | bytes 3244040 | tf_op jit(solution)/shard_map/ppermute | solution.py:66
  145.7 49.5 %collective-permute-start.12 = (bf16[128,4224]{1,0:T(8,128)(2,1)S(1)}, bf16[128,4224]{1,0:T(8,128)(2,1)S(1)}, u32[]{:S(2)}, u32[]{:S(2)}) collective-permute-start(bf16[128,4224]{1,0:T(8,128)(2,1)S(1)} %pad_maximum_fusion.2), channel_id=1, source_target_pairs={{0,192},{64,0},{128,64},{192,128},{1,193},{65,1},{129,65},{193,129... | collective-permute-start | bytes 3244040 | tf_op jit(solution)/shard_map/ppermute | solution.py:66
  198.4 40.3 %all-to-all-start.2 = ((bf16[2,64,4224]{2,0,1:T(2,128)(2,1)}), bf16[2,64,4224]{2,0,1:T(2,128)(2,1)}, u32[]{:S(2)}, u32[]{:S(2)}) async-start(bf16[2,64,4224]{2,0,1:T(2,128)(2,1)} %copy.28), calls=%async_computation.2 | async-start | bytes 2162688 | tf_op jit(solution)/shard_map/all_to_all | solution.py:103
  209.5 1.2 copy-start.2
  210.7 1.2 copy-start.4
  212.0 1.2 copy-start.6
  213.2 1.2 copy-start.8
  218.2 23.0 %copy-start.18 = (f32[8,8,64]{2,1,0:T(8,128)S(1)}, f32[8,8,64]{2,1,0:T(8,128)}, u32[]{:S(2)}) copy-start(f32[8,8,64]{2,1,0:T(8,128)} %copy-done.17) | copy-start | bytes 49156
